TPU v7x, 256 devices: a whole 4x4x8 slice. The times are simulated.
256 devices in a mesh: ctx: 64 (over z, x, core), exp: 4 (over y).
Axes of the slice: x: 4, y: 4, z: 8, core: 2. Of those that a mesh axis runs over, the one named last changes fastest.
Arguments:
- queries: bfloat16 [16384, 4096], P('ctx', 'exp'), may hold values from -6 to 6
- keys: bfloat16 [16384, 4096], P('ctx', 'exp'), may hold values from -6 to 6
- values: bfloat16 [16384, 4096], P('ctx', 'exp'), may hold values from -6 to 6
- gates: bfloat16 [16384, 4096], P('ctx', 'exp'), may hold values from -6 to 6
- decay_rate: float32 [32], P('exp'), may hold values from 1.2207031e-06 to 0.05
- norm_gain: float32 [4096], P('exp'), may hold values from 0.1 to 1.9
- moe_rows: bfloat16 [2048, 3072], P('exp'), may hold values from -6 to 6
- tile_expert: int32 [16, 1], P('exp'), may hold values from 0 to 3; in each aligned block of 4 rows (0 to 3, 4 to 7, ...) at most 2 rows name the same one
- row_weight: float32 [2048], P('exp'), may hold values from 0.2 to 1
- w_gate: bfloat16 [4, 3072, 9216], P('exp', None, 'ctx'), may hold values from -0.109375 to 0.109375
- w_up: bfloat16 [4, 3072, 9216], P('exp', None, 'ctx'), may hold values from -0.109375 to 0.109375
- w_down: bfloat16 [4, 9216, 3072], P('exp', 'ctx'), may hold values from -0.1875 to 0.1875
Outputs:
- attention_out: bfloat16 [16384, 4096], P('ctx', 'exp')
- moe_out: bfloat16 [2048, 3072], P('exp', 'ctx')
Inputs may be any that keep to these rules, and one draw needn't show every extreme that they name: `tile_expert`: among the 4 tiles of one index of exp at most 2 name the same expert, and some index has exactly 2 tiles for one expert.
All inputs are finite; a program needn't handle non-finite values.
Results may differ from a plain program's by a relative error of at most 0.0057.
Values may be sent and summed in bfloat16 or wider, within the bound.
No kernel may reach another device: no remote copies, remote signals or barrier semaphores. Data moves between devices by JAX's collectives and lax.ppermute only.
A program may use at most 128 MiB of HBM per device.

v0:
```python
import functools

import jax
import jax.numpy as jnp
from jax import lax
from jax.experimental import pallas as pl
from jax.experimental.pallas import tpu as pltpu
from jax.sharding import Mesh
from jax.sharding import PartitionSpec as P

BF = jnp.bfloat16
F32 = jnp.float32
CTX = ("z", "x", "core")
HEAD = 128
TILE = 128
GROUP = 4
LAST = 1


def _state_kernel(rate, k, v, out):
    tokens = k.shape[0]
    first = pl.program_id(0) * GROUP
    t = lax.broadcasted_iota(jnp.int32, (tokens, HEAD), 0).astype(F32)
    for h in range(GROUP):
        at = slice(h * HEAD, (h + 1) * HEAD)
        decay = jnp.exp(-rate[first + h] * (tokens - t))
        scaled = (k[:, at].astype(F32) * decay).astype(BF)
        out[at, :] = lax.dot_general(
            scaled, v[:, at], (((0,), (0,)), ((), ())), preferred_element_type=F32
        ).astype(BF)


def local_states(rate, keys, values):
    tokens, width = keys.shape
    spec = pl.BlockSpec((tokens, GROUP * HEAD), lambda h: (0, h))
    return pl.pallas_call(
        _state_kernel,
        grid=(width // (GROUP * HEAD),),
        in_specs=[pl.BlockSpec(memory_space=pltpu.SMEM), spec, spec],
        out_specs=pl.BlockSpec((GROUP * HEAD, HEAD), lambda h: (h, 0)),
        out_shape=jax.ShapeDtypeStruct((width, HEAD), BF),
        compiler_params=pltpu.CompilerParams(vmem_limit_bytes=8 << 20),
        name="local_states",
    )(rate, keys, values)


def _scan_kernel(tokens, heads, rate, states, out):
    blocks, rows, width = states.shape
    mine = lax.axis_index(CTX) * heads // blocks
    lam = jnp.exp(jnp.full((rows, width), -rate[mine] * tokens, F32))
    carry = jnp.zeros((rows, width), F32)
    for b in range(blocks):
        out[b] = carry.astype(BF)
        carry = carry * lam + states[b].astype(F32)


def scan_states(tokens, rate, states):
    return pl.pallas_call(
        functools.partial(_scan_kernel, tokens, rate.shape[0]),
        in_specs=[
            pl.BlockSpec(memory_space=pltpu.SMEM),
            pl.BlockSpec(memory_space=pltpu.VMEM),
        ],
        out_specs=pl.BlockSpec(memory_space=pltpu.VMEM),
        out_shape=jax.ShapeDtypeStruct(states.shape, BF),
        compiler_params=pltpu.CompilerParams(vmem_limit_bytes=6 << 20),
        name="scan_states",
    )(rate, states)


def _intra_kernel(rate, q, k, v, out):
    tokens = q.shape[0]
    first = pl.program_id(0) * GROUP
    i = lax.broadcasted_iota(jnp.int32, (tokens, tokens), 0)
    j = lax.broadcasted_iota(jnp.int32, (tokens, tokens), 1)
    off = (i - j).astype(F32)
    for h in range(GROUP):
        at = slice(h * HEAD, (h + 1) * HEAD)
        r = rate[first + h]
        within = jnp.where(off >= 0.0, jnp.exp(-r * jnp.maximum(off, 0.0)), 0.0)
        scores = lax.dot_general(
            q[:, at], k[:, at], (((1,), (1,)), ((), ())), preferred_element_type=F32
        )
        out[:, at] = jnp.dot(
            (scores * within).astype(BF), v[:, at], preferred_element_type=F32
        )


def intra_part(rate, queries, keys, values):
    tokens, width = keys.shape
    spec = pl.BlockSpec((tokens, GROUP * HEAD), lambda h: (0, h))
    return pl.pallas_call(
        _intra_kernel,
        grid=(width // (GROUP * HEAD),),
        in_specs=[pl.BlockSpec(memory_space=pltpu.SMEM), spec, spec, spec],
        out_specs=spec,
        out_shape=jax.ShapeDtypeStruct((tokens, width), F32),
        compiler_params=pltpu.CompilerParams(vmem_limit_bytes=14 << 20),
        name="intra_part",
    )(rate, queries, keys, values)


def _mix_kernel(rate, intra, q, prefix, mixed, squares):
    tokens = q.shape[0]
    step = pl.program_id(0)
    t = lax.broadcasted_iota(jnp.int32, (tokens, HEAD), 0).astype(F32)
    total = jnp.zeros((tokens, HEAD), F32)
    for h in range(GROUP):
        at = slice(h * HEAD, (h + 1) * HEAD)
        r = rate[step * GROUP + h]
        inter = jnp.dot(q[:, at], prefix[at, :], preferred_element_type=F32)
        value = intra[:, at] + inter * jnp.exp(-r * t)
        mixed[:, at] = value
        total += value * value

    @pl.when(step == 0)
    def _():
        squares[...] = jnp.zeros_like(squares)

    squares[...] += jnp.sum(jnp.transpose(total), axis=0, keepdims=True)


def mix_part(rate, intra, queries, prefix):
    tokens, width = queries.shape
    spec = pl.BlockSpec((tokens, GROUP * HEAD), lambda h: (0, h))
    return pl.pallas_call(
        _mix_kernel,
        grid=(width // (GROUP * HEAD),),
        in_specs=[
            pl.BlockSpec(memory_space=pltpu.SMEM),
            spec,
            spec,
            pl.BlockSpec((GROUP * HEAD, HEAD), lambda h: (h, 0)),
        ],
        out_specs=[spec, pl.BlockSpec((1, tokens), lambda h: (0, 0))],
        out_shape=[
            jax.ShapeDtypeStruct((tokens, width), F32),
            jax.ShapeDtypeStruct((1, tokens), F32),
        ],
        compiler_params=pltpu.CompilerParams(vmem_limit_bytes=14 << 20),
        name="mix_part",
    )(rate, intra, queries, prefix)


def _norm_kernel(features, *refs):
    *squares, mixed, gain, gates, out = refs
    tokens = mixed.shape[0]
    total = sum((part[...] for part in squares[1:]), squares[0][...])
    factor = lax.rsqrt(total / features + 1e-06)
    column = jnp.transpose(jnp.broadcast_to(factor, (HEAD, tokens)))
    for h in range(GROUP):
        at = slice(h * HEAD, (h + 1) * HEAD)
        scaled = mixed[:, at] * column * gain[:, at]
        out[:, at] = (scaled * jax.nn.sigmoid(gates[:, at].astype(F32))).astype(BF)


def norm_part(features, squares, mixed, gain, gates):
    tokens, width = mixed.shape
    spec = pl.BlockSpec((tokens, GROUP * HEAD), lambda h: (0, h))
    row = pl.BlockSpec((1, tokens), lambda h: (0, 0))
    return pl.pallas_call(
        functools.partial(_norm_kernel, features),
        grid=(width // (GROUP * HEAD),),
        in_specs=[row] * len(squares)
        + [spec, pl.BlockSpec((1, GROUP * HEAD), lambda h: (0, h)), spec],
        out_specs=spec,
        out_shape=jax.ShapeDtypeStruct((tokens, width), BF),
        compiler_params=pltpu.CompilerParams(vmem_limit_bytes=14 << 20),
        name="norm_part",
    )(*squares, mixed, gain, gates)


def _pick_kernel(ids, rows, *refs):
    outs, held, into, out_of = refs[:-3], refs[-3], refs[-2], refs[-1]
    n_exp, me_e, me_core = lax.axis_size("exp"), lax.axis_index("exp"), lax.axis_index("core")
    tiles, half = ids.shape[0], TILE // 2
    loads = []
    for k in range(len(outs)):
        target = lax.rem(me_e + k + 1, n_exp)
        seen = jnp.int32(0)
        tile = [jnp.int32(0), jnp.int32(0)]
        for t in range(tiles):
            same = ids[t] == target
            for rank in range(2):
                tile[rank] = jnp.where(same & (seen == rank), t, tile[rank])
            seen = seen + same.astype(jnp.int32)
        for rank in range(2):
            start = pl.multiple_of(tile[rank] * TILE + me_core * half, half)
            load = pltpu.make_async_copy(
                rows.at[pl.ds(start, half), :],
                held.at[k, pl.ds(rank * half, half), :],
                into.at[k, rank],
            )
            load.start()
            loads.append(load)
    stores = []
    for k in range(len(outs)):
        loads[2 * k].wait()
        loads[2 * k + 1].wait()
        store = pltpu.make_async_copy(held.at[k], outs[k], out_of.at[k])
        store.start()
        stores.append(store)
    for store in stores:
        store.wait()


def pick_tiles(ids, rows, count):
    tile = jax.ShapeDtypeStruct((TILE, rows.shape[1]), rows.dtype)
    return pl.pallas_call(
        _pick_kernel,
        in_specs=[
            pl.BlockSpec(memory_space=pltpu.SMEM),
            pl.BlockSpec(memory_space=pl.ANY),
        ],
        out_specs=[pl.BlockSpec(memory_space=pl.ANY)] * count,
        out_shape=[tile] * count,
        scratch_shapes=[
            pltpu.VMEM((count, TILE, rows.shape[1]), rows.dtype),
            pltpu.SemaphoreType.DMA((count, 2)),
            pltpu.SemaphoreType.DMA((count,)),
        ],
        compiler_params=pltpu.CompilerParams(vmem_limit_bytes=58 << 20),
        name="pick_tiles",
    )(ids, rows)


def _hidden_kernel(count, *refs):
    sources, out = refs[: count + 4], refs[count + 4]
    rows, weights, sems = refs[count + 5 :]
    units = weights.shape[0] // 4
    targets = [rows.at[i * TILE : (i + 1) * TILE, :] for i in range(count)]
    targets += [weights.at[i * units : (i + 1) * units, :] for i in range(4)]
    copies = [
        pltpu.make_async_copy(source, target, sems.at[i])
        for i, (source, target) in enumerate(zip(sources, targets))
    ]
    order = list(range(count, count + 4)) + list(range(count))
    for i in order:
        copies[i].start()
    for i in range(4):
        copies[count + i].wait()
    dims = (((1,), (1,)), ((), ()))
    wide = 2 * TILE
    for j in range(count // 2):
        copies[2 * j].wait()
        copies[2 * j + 1].wait()
        at = slice(j * wide, (j + 1) * wide)
        both = lax.dot_general(
            weights[...], rows[at, :], dims, preferred_element_type=F32
        )
        gate, up = both[: 2 * units], both[2 * units :]
        out[:, at] = (jax.nn.silu(gate) * up).astype(BF)


def hidden_part(rows, weights):
    count, (units, model) = len(rows), weights[0].shape
    return pl.pallas_call(
        functools.partial(_hidden_kernel, count),
        in_specs=[pl.BlockSpec(memory_space=pl.ANY)] * (count + 4),
        out_specs=pl.BlockSpec(memory_space=pltpu.VMEM),
        out_shape=jax.ShapeDtypeStruct((2 * units, count * TILE), BF),
        scratch_shapes=[
            pltpu.VMEM((count * TILE, model), BF),
            pltpu.VMEM((4 * units, model), BF),
            pltpu.SemaphoreType.DMA((count + 4,)),
        ],
        compiler_params=pltpu.CompilerParams(vmem_limit_bytes=58 << 20),
        name="hidden_part",
    )(*rows, *weights)


def _split_kernel(n_z, weight, *outs):
    me_x, n_x = lax.axis_index("x"), len(outs)
    units, window = weight.shape[0], weight.shape[1] // n_z
    own = window // n_x
    lane = lax.broadcasted_iota(jnp.int32, (units, window), 1)
    for g in range(n_z // n_x):
        parts = [
            weight[:, z * window : (z + 1) * window].astype(F32)
            for z in range(g * n_x, (g + 1) * n_x)
        ]
        for k, out in enumerate(outs):
            target = lax.rem(me_x + k, n_x)
            total = jnp.zeros((units, window), F32)
            for i, part in enumerate(parts):
                turn = lax.rem(i + n_x - target, n_x) * own
                here = (lane >= i * own) & (lane < (i + 1) * own)
                total = jnp.where(here, pltpu.roll(part, turn, 1), total)
            out[:, g * window : (g + 1) * window] = total.astype(BF)


def split_columns(weight, n_z, n_x):
    units, model = weight.shape
    vmem = pl.BlockSpec(memory_space=pltpu.VMEM)
    return pl.pallas_call(
        functools.partial(_split_kernel, n_z),
        in_specs=[vmem],
        out_specs=[vmem] * n_x,
        out_shape=[jax.ShapeDtypeStruct((units, model // n_x), BF)] * n_x,
        compiler_params=pltpu.CompilerParams(vmem_limit_bytes=14 << 20),
        name="split_columns",
    )(weight)


def _stack_kernel(*refs):
    parts, out, sems = refs[:-2], refs[-2], refs[-1]
    units = parts[0].shape[0]
    copies = [
        pltpu.make_async_copy(part, out.at[i * units : (i + 1) * units, :], sems.at[i])
        for i, part in enumerate(parts)
    ]
    for copy in copies:
        copy.start()
    for copy in copies:
        copy.wait()


def stack_rows(parts):
    units, chunk = parts[0].shape
    return pl.pallas_call(
        _stack_kernel,
        in_specs=[pl.BlockSpec(memory_space=pl.ANY)] * len(parts),
        out_specs=pl.BlockSpec(memory_space=pltpu.VMEM),
        out_shape=jax.ShapeDtypeStruct((len(parts) * units, chunk), BF),
        scratch_shapes=[pltpu.SemaphoreType.DMA((len(parts),))],
        compiler_params=pltpu.CompilerParams(vmem_limit_bytes=10 << 20),
        name="stack_rows",
    )(*parts)


def _down_kernel(weight, *refs):
    hidden, out, held = refs[:-2], refs[-2], refs[-1]
    units = hidden[0].shape[0]
    for k, part in enumerate(hidden):
        held[k * units : (k + 1) * units, :] = part[...]
    blocks, slots, columns = out.shape[:3]
    me_e = lax.axis_index("exp")
    total = lax.dot_general(
        weight[...], held[...], (((0,), (0,)), ((), ())), preferred_element_type=F32
    ).astype(BF)
    for slot in range(slots):
        home = lax.rem(me_e + slots - slot, slots)
        block = total[:, slot * TILE : (slot + 1) * TILE]
        out[:, home] = block.reshape(blocks, columns, TILE)


def down_part(weight, hidden, blocks, columns):
    rows = hidden[0].shape[1]
    vmem = pl.BlockSpec(memory_space=pltpu.VMEM)
    return pl.pallas_call(
        _down_kernel,
        in_specs=[vmem] * (1 + len(hidden)),
        out_specs=vmem,
        out_shape=jax.ShapeDtypeStruct((blocks, rows // TILE, columns, TILE), BF),
        scratch_shapes=[pltpu.VMEM((weight.shape[0], rows), BF)],
        compiler_params=pltpu.CompilerParams(vmem_limit_bytes=24 << 20),
        name="down_part",
    )(weight, *hidden)


def _finish_kernel(ids, parts, weight, out):
    n_z, n_core, n_exp, columns, _ = parts.shape
    tiles, half = ids.shape[0], TILE // 2
    low = lax.broadcasted_iota(jnp.int32, (columns, TILE), 1) < half
    for t in range(tiles):
        rank = jnp.int32(0)
        for earlier in range(t):
            rank = rank + (ids[earlier] == ids[t]).astype(jnp.int32)
        sums = []
        for core in range(n_core):
            total = jnp.zeros((columns, TILE), F32)
            for z in range(n_z):
                total = total + parts[z, core, ids[t]].astype(F32)
            sums.append(total.astype(BF).astype(F32))
        first, second = sums
        zero = jnp.where(low, first, pltpu.roll(second, half, 1))
        one = jnp.where(low, pltpu.roll(first, half, 1), second)
        rows = jnp.where(rank == 0, zero, one)
        at = slice(t * TILE, (t + 1) * TILE)
        out[:, at] = (rows * weight[:, at]).astype(BF)


def finish_part(ids, parts, weight):
    columns = parts.shape[3]
    vmem = pl.BlockSpec(memory_space=pltpu.VMEM)
    return pl.pallas_call(
        _finish_kernel,
        in_specs=[pl.BlockSpec(memory_space=pltpu.SMEM), vmem, vmem],
        out_specs=vmem,
        out_shape=jax.ShapeDtypeStruct((columns, weight.shape[1]), BF),
        compiler_params=pltpu.CompilerParams(vmem_limit_bytes=8 << 20),
        name="finish_part",
    )(ids, parts, weight)


def shift(array, axis, by):
    n = lax.axis_size(axis)
    return lax.ppermute(array, axis, [(i, (i + by) % n) for i in range(n)])


def on_device(
    queries, keys, values, gates, decay_rate, norm_gain,
    moe_rows, tile_expert, row_weight, w_gate, w_up, w_down,
):
    n_exp, n_z = lax.axis_size("exp"), lax.axis_size("z")
    n_x, n_core = lax.axis_size("x"), lax.axis_size("core")
    n_ctx = n_z * n_x * n_core
    tokens, width = queries.shape
    model = moe_rows.shape[1]
    ids = tile_expert[:, 0]
    columns = model // n_ctx

    gate_own = jnp.swapaxes(w_gate[0], 0, 1)
    up_own = jnp.swapaxes(w_up[0], 0, 1)
    gate_other = shift(gate_own, "core", 1)
    up_other = shift(up_own, "core", 1)
    units = gate_own.shape[0]

    picked = pick_tiles(ids, moe_rows, n_exp)
    *picked, keys_late = lax.optimization_barrier((*picked, keys))
    arrived = [picked[-1]]
    arrived += [shift(picked[k - 1], "exp", k) for k in range(1, n_exp)]
    gate_other, up_other, keys_late = lax.optimization_barrier(
        (gate_other, up_other, keys_late)
    )

    states = local_states(decay_rate, keys_late, values)
    states, w_down = lax.optimization_barrier((states, w_down))
    pieces = states.reshape(n_ctx, width // n_ctx, HEAD)
    pieces = lax.all_to_all(pieces, CTX, 0, 0, tiled=True)
    pieces = scan_states(float(tokens), decay_rate, pieces)
    chunks = list(split_columns(w_down[0], n_z, n_x))
    down_own, down_other = [chunks[0]] + [None] * (n_x - 1), [None] * n_x
    lanes = (
        (("x", 1), ("x", 3), ("core", 1), ("core", 3)),
        (("x", 2), ("core", 0), ("core", 2)),
    )
    for lane in lanes:
        last = None
        for axis, k in lane:
            part = chunks[k] if axis == "x" else down_own[k]
            if last is not None and last is not part:
                part, last = lax.optimization_barrier((part, last))
            last = shift(part, axis, k if axis == "x" else 1)
            if axis == "x":
                down_own[k] = last
            else:
                down_other[k] = last
    arrived[LAST], _ = lax.optimization_barrier((arrived[LAST], pieces))

    weights = (gate_own, gate_other, up_own, up_other)
    hidden = hidden_part(arrived, weights)
    hidden, queries = lax.optimization_barrier((hidden, queries))
    hidden = [hidden] + [shift(hidden, "x", k) for k in range(1, n_x)]
    intra = intra_part(decay_rate, queries, keys, values)
    hidden[1], intra = lax.optimization_barrier((hidden[1], intra))
    prefix = lax.all_to_all(pieces, CTX, 0, 0, tiled=True).reshape(width, HEAD)
    down = stack_rows([part for pair in zip(down_own, down_other) for part in pair])
    hidden[2], down = lax.optimization_barrier((hidden[2], down))
    parts = down_part(down, hidden, n_z * n_core, columns)
    parts, prefix = lax.optimization_barrier((parts, prefix))
    parts = parts.reshape(-1, columns, TILE)
    parts = lax.all_to_all(parts, ("z", "core", "exp"), 0, 0, tiled=True)
    parts = parts.reshape(n_z, n_core, n_exp, columns, TILE)

    mixed, squares = mix_part(decay_rate, intra, queries, prefix)
    squares = [lax.psum(squares, "exp")]
    attention_out = norm_part(
        float(width * n_exp), squares, mixed, norm_gain[None, :], gates
    )
    moe_out = jnp.swapaxes(finish_part(ids, parts, row_weight[None, :]), 0, 1)
    return attention_out, moe_out


def solution(mesh):
    n_core, n_x = 2, 4
    grid = mesh.devices.reshape(-1, n_x, n_core, mesh.devices.shape[1])
    fine = Mesh(grid, ("z", "x", "core", "exp"))
    placed = (
        P(CTX, "exp"),
        P(CTX, "exp"),
        P(CTX, "exp"),
        P(CTX, "exp"),
        P("exp"),
        P("exp"),
        P("exp", None),
        P("exp", None),
        P("exp"),
        P("exp", None, CTX),
        P("exp", None, CTX),
        P("exp", CTX, None),
    )
    return jax.shard_map(
        on_device,
        mesh=fine,
        in_specs=placed,
        out_specs=(P(CTX, "exp"), P("exp", CTX)),
        check_vma=False,
    )
```

profile of v0, /device:TPU:6, one launch (start us, length us, event | category | flops | bytes accessed | tf_op | source)
XLA Modules:
  0.0 109.0 jit_solution(2162583629552735536)
XLA Ops:
  0.8 0.5 collective-permute-start.2
  1.3 4.4 %pick_tiles.1 = (bf16[128,3072]{1,0:T(8,128)(2,1)}, bf16[128,3072]{1,0:T(8,128)(2,1)}, bf16[128,3072]{1,0:T(8,128)(2,1)}, bf16[128,3072]{1,0:T(8,128)(2,1)}) custom-call(s32[4]{0:T(128)} %bitcast.20, bf16[512,3072]{1,0:T(8,128)(2,1)} %rows.1), custom_call_target="tpu_custom_call" | custom-call | tf_op jit(solution)/shard_map/pick_tiles/pallas_call | solution.py:209
  5.7 1.7 %collective-permute-start = (bf16[128,3072]{1,0:T(8,128)(2,1)}, bf16[128,3072]{1,0:T(8,128)(2,1)}, u32[]{:S(2)}, u32[]{:S(2)}) collective-permute-start(bf16[128,3072]{1,0:T(8,128)(2,1)} %get-tuple-element.41), channel_id=1, source_target_pairs={{0,1},{1,2},{2,3},{3,0},{4,5},{5,6},{6,7},{7,4},{8,9},{9,10},{10,1... | collective-permute-start | bytes 2359304 | tf_op jit(solution)/shard_map/ppermute | solution.py:398
  7.4 2.9 %collective-permute-start.3 = (bf16[128,3072]{1,0:T(8,128)(2,1)}, bf16[128,3072]{1,0:T(8,128)(2,1)}, u32[]{:S(2)}, u32[]{:S(2)}) collective-permute-start(bf16[128,3072]{1,0:T(8,128)(2,1)} %get-tuple-element.46), channel_id=1, source_target_pairs={{0,2},{1,3},{2,0},{3,1},{4,6},{5,7},{6,4},{7,5},{8,10},{9,11},{10,... | collective-permute-start | bytes 2359304 | tf_op jit(solution)/shard_map/ppermute | solution.py:398
  10.3 1.4 %collective-permute-start.4 = (bf16[128,3072]{1,0:T(8,128)(2,1)}, bf16[128,3072]{1,0:T(8,128)(2,1)}, u32[]{:S(2)}, u32[]{:S(2)}) collective-permute-start(bf16[128,3072]{1,0:T(8,128)(2,1)} %get-tuple-element.47), channel_id=1, source_target_pairs={{0,3},{1,0},{2,1},{3,2},{4,7},{5,4},{6,5},{7,6},{8,11},{9,8},{10,9... | collective-permute-start | bytes 2359304 | tf_op jit(solution)/shard_map/ppermute | solution.py:398
  11.7 1.9 %local_states.1 = bf16[1024,128]{1,0:T(8,128)(2,1)} custom-call(f32[8]{0:T(128)S(1)} %copy-done.8, bf16[256,1024]{1,0:T(8,128)(2,1)S(1)} %copy-done, bf16[256,1024]{1,0:T(8,128)(2,1)S(1)} %copy-done.1), custom_call_target="tpu_custom_call" | custom-call | tf_op jit(solution)/shard_map/local_states/pallas_call | solution.py:36
  13.6 12.0 %all-to-all-start = ((bf16[64,16,128]{2,1,0:T(8,128)(2,1)}), bf16[64,16,128]{2,1,0:T(8,128)(2,1)S(1)}, u32[]{:S(2)}, u32[]{:S(2)}) async-start(bf16[64,16,128]{2,1,0:T(8,128)(2,1)} %bitcast.5), calls=%async_computation | async-start | bytes 524288 | tf_op jit(solution)/shard_map/all_to_all | solution.py:430
  25.6 1.9 %split_columns.1 = (bf16[144,768]{1,0:T(8,128)(2,1)S(1)}, bf16[144,768]{1,0:T(8,128)(2,1)S(1)}, bf16[144,768]{1,0:T(8,128)(2,1)}, bf16[144,768]{1,0:T(8,128)(2,1)S(1)}) custom-call(bf16[144,3072]{1,0:T(8,128)(2,1)S(1)} %bitcast.17), custom_call_target="tpu_custom_call" | custom-call | tf_op jit(solution)/shard_map/split_columns/pallas_call | solution.py:295
  27.5 0.5 collective-permute-start.9
  27.9 2.5 %collective-permute-start.7 = (bf16[144,768]{1,0:T(8,128)(2,1)}, bf16[144,768]{1,0:T(8,128)(2,1)S(1)}, u32[]{:S(2)}, u32[]{:S(2)}) collective-permute-start(bf16[144,768]{1,0:T(8,128)(2,1)} %get-tuple-element.55), channel_id=1, source_target_pairs={{0,16},{8,24},{16,0},{24,8},{1,17},{9,25},{17,1},{25,9},{2,18},{10... | collective-permute-start | bytes 663560 | tf_op jit(solution)/shard_map/ppermute | solution.py:398
  30.4 7.2 %collective-permute-done.9.refs_2_ = bf16[144,768]{1,0:T(8,128)(2,1)S(1)} collective-permute-done((bf16[144,768]{1,0:T(8,128)(2,1)S(1)}, bf16[144,768]{1,0:T(8,128)(2,1)S(1)}, u32[]{:S(2)}, u32[]{:S(2)}) %collective-permute-start.9) | collective-permute-done | bytes 221216 | tf_op jit(solution)/shard_map/ppermute | solution.py:398
  37.6 0.6 collective-permute-start.10
  38.2 1.4 %scan_states.1 = bf16[64,16,128]{2,1,0:T(8,128)(2,1)} custom-call(f32[8]{0:T(128)S(1)} %copy-done.8, bf16[64,16,128]{2,1,0:T(8,128)(2,1)S(1)} %all-to-all-done.states), custom_call_target="tpu_custom_call" | custom-call | tf_op jit(solution)/shard_map/scan_states/pallas_call | solution.py:58
  39.6 9.1 %all-to-all-start.1 = ((bf16[64,16,128]{2,1,0:T(8,128)(2,1)}), bf16[64,16,128]{2,1,0:T(8,128)(2,1)S(1)}, u32[]{:S(2)}, u32[]{:S(2)}) async-start(bf16[64,16,128]{2,1,0:T(8,128)(2,1)} %scan_states.1), calls=%async_computation.1 | async-start | bytes 524288 | tf_op jit(solution)/shard_map/all_to_all | solution.py:457
  49.0 0.4 collective-permute-start.11
  49.4 7.2 %hidden_part.1.refs_0_ = bf16[288,512]{1,0:T(8,128)(2,1)} custom-call(bf16[128,3072]{1,0:T(8,128)(2,1)} %get-tuple-element.40.refs_0_, bf16[128,3072]{1,0:T(8,128)(2,1)} %collective-permute-done.refs_1_, bf16[128,3072]{1,0:T(8,128)(2,1)} %collective-permute-done.3.refs_2_, bf16[128,3072]{1,0:T(8,128)(2,1)} %collective-permute-done.4.refs_3_, ...), custom_call_target="tpu_custom_call" | custom-call | tf_op jit(solution)/shard_map/hidden_part/pallas_call | solution.py:257
  56.6 0.5 collective-permute-start.5
  57.2 2.5 %collective-permute-start.6 = (bf16[288,512]{1,0:T(8,128)(2,1)}, bf16[288,512]{1,0:T(8,128)(2,1)S(1)}, u32[]{:S(2)}, u32[]{:S(2)}) collective-permute-start(bf16[288,512]{1,0:T(8,128)(2,1)} %hidden_part.1.refs_0_), channel_id=1, source_target_pairs={{0,16},{8,24},{16,0},{24,8},{1,17},{9,25},{17,1},{25,9},{2,18},{10... | collective-permute-start | bytes 884744 | tf_op jit(solution)/shard_map/ppermute | solution.py:398
  59.7 0.5 collective-permute-start.13
  60.2 2.0 %intra_part.1.intra = f32[256,1024]{1,0:T(8,128)S(1)} custom-call(f32[8]{0:T(128)S(1)} %copy-done.8, bf16[256,1024]{1,0:T(8,128)(2,1)S(1)} %copy-done.2, bf16[256,1024]{1,0:T(8,128)(2,1)S(1)} %copy-done, bf16[256,1024]{1,0:T(8,128)(2,1)S(1)} %copy-done.1), custom_call_target="tpu_custom_call" | custom-call | tf_op jit(solution)/shard_map/intra_part/pallas_call | solution.py:92
  62.2 4.6 %collective-permute-done.5.refs_1_ = bf16[288,512]{1,0:T(8,128)(2,1)S(1)} collective-permute-done((bf16[288,512]{1,0:T(8,128)(2,1)}, bf16[288,512]{1,0:T(8,128)(2,1)S(1)}, u32[]{:S(2)}, u32[]{:S(2)}) %collective-permute-start.5) | collective-permute-done | bytes 294944 | tf_op jit(solution)/shard_map/ppermute | solution.py:398
  66.8 2.7 %stack_rows.1.weight = bf16[1152,768]{1,0:T(8,128)(2,1)S(1)} custom-call(bf16[144,768]{1,0:T(8,128)(2,1)S(1)} %get-tuple-element.56.refs_0_, bf16[144,768]{1,0:T(8,128)(2,1)S(1)} %collective-permute-done.8.refs_1_, bf16[144,768]{1,0:T(8,128)(2,1)S(1)} %collective-permute-done.9.refs_2_, bf16[144,768]{1,0:T(8,128)(2,1)S(1)} %collective-permute-done.11.refs_3_, ...), custom_call_target="tpu_custom_call" | custom-call | tf_op jit(solution)/shard_map/stack_rows/pallas_call | solution.py:320
  69.5 4.6 %collective-permute-done.14.refs_3_ = bf16[288,512]{1,0:T(8,128)(2,1)S(1)} collective-permute-done((bf16[288,512]{1,0:T(8,128)(2,1)}, bf16[288,512]{1,0:T(8,128)(2,1)S(1)}, u32[]{:S(2)}, u32[]{:S(2)}) %collective-permute-start.14) | collective-permute-done | bytes 294944 | tf_op jit(solution)/shard_map/ppermute | solution.py:398
  74.1 2.1 %down_part.1 = bf16[16,4,48,128]{3,2,1,0:T(8,128)(2,1)} custom-call(bf16[1152,768]{1,0:T(8,128)(2,1)S(1)} %stack_rows.1.weight, bf16[288,512]{1,0:T(8,128)(2,1)S(1)} %copy-done.3, bf16[288,512]{1,0:T(8,128)(2,1)S(1)} %collective-permute-done.5.refs_1_, bf16[288,512]{1,0:T(8,128)(2,1)S(1)} %collective-permute-done.6.refs_2_, ...), custom_call_target="tpu_custom_call" | custom-call | tf_op jit(solution)/shard_map/down_part/pallas_call | solution.py:350
  76.2 8.1 %all-to-all-start.2 = ((bf16[64,48,128]{2,1,0:T(8,128)(2,1)}), bf16[64,48,128]{2,1,0:T(8,128)(2,1)S(1)}, u32[]{:S(2)}, u32[]{:S(2)}) async-start(bf16[64,48,128]{2,1,0:T(8,128)(2,1)} %bitcast.9), calls=%async_computation.2 | async-start | bytes 1572864 | tf_op jit(solution)/shard_map/all_to_all | solution.py:463
  84.3 1.3 %mix_part.1 = (f32[256,1024]{1,0:T(8,128)S(1)}, f32[1,256]{1,0:T(1,128)S(1)}) custom-call(f32[8]{0:T(128)S(1)} %copy-done.8, f32[256,1024]{1,0:T(8,128)S(1)} %intra_part.1.intra, bf16[256,1024]{1,0:T(8,128)(2,1)S(1)} %copy-done.2, bf16[1024,128]{1,0:T(8,128)(2,1)S(1)} %bitcast.16), custom_call_target="tpu_custom_call" | custom-call | tf_op jit(solution)/shard_map/mix_part/pallas_call | solution.py:126
  85.7 1.0 copy-done.4
  86.7 10.5 %psum.7.refs_0_ = f32[1,256]{1,0:T(1,128)S(1)} all-reduce(f32[1,256]{1,0:T(1,128)S(1)} %get-tuple-element.67), channel_id=1, replica_groups=mesh['z'=8,'x'=4,'core'=2,'exp'=4] {'exp'}, use_global_device_ids=true, to_apply=%region_0.0 | all-reduce | flops 256 | bytes 2048 | tf_op jit(solution)/shard_map/psum | solution.py:467
  97.2 1.2 %copy-done.5 = f32[256,1024]{1,0:T(8,128)S(1)} copy-done((f32[256,1024]{1,0:T(8,128)S(1)}, f32[256,1024]{1,0:T(8,128)}, u32[]{:S(2)}) %copy-start.5) | copy-done | bytes 1048600
  98.4 1.2 %norm_part.1 = bf16[256,1024]{1,0:T(8,128)(2,1)} custom-call(f32[1,256]{1,0:T(1,128)S(1)} %psum.7.refs_0_, f32[256,1024]{1,0:T(8,128)S(1)} %copy-done.5, f32[1,1024]{1,0:T(1,128)S(1)} %bitcast.18, bf16[256,1024]{1,0:T(8,128)(2,1)S(1)} %copy-done.7), custom_call_target="tpu_custom_call" | custom-call | tf_op jit(solution)/shard_map/norm_part/pallas_call | solution.py:161
  99.6 8.1 %all-to-all-done.2 = bf16[64,48,128]{2,1,0:T(8,128)(2,1)S(1)} async-done(((bf16[64,48,128]{2,1,0:T(8,128)(2,1)}), bf16[64,48,128]{2,1,0:T(8,128)(2,1)S(1)}, u32[]{:S(2)}, u32[]{:S(2)}) %all-to-all-start.2) | async-done | bytes 786464 | tf_op jit(solution)/shard_map/all_to_all | solution.py:463
  107.7 1.3 %finish_part.1 = bf16[48,512]{1,0:T(8,128)(2,1)} custom-call(s32[4]{0:T(128)S(1)} %bitcast.21, bf16[8,2,4,48,128]{4,3,2,1,0:T(8,128)(2,1)S(1)} %bitcast.15, f32[1,512]{1,0:T(1,128)S(1)} %bitcast.19), custom_call_target="tpu_custom_call" | custom-call | tf_op jit(solution)/shard_map/finish_part/pallas_call | solution.py:386
  (42 shorter events, 0.4 us)
Async XLA Ops:
  0.6 11.0 %copy-start = (bf16[256,1024]{1,0:T(8,128)(2,1)S(1)}, bf16[256,1024]{1,0:T(8,128)(2,1)}, u32[]{:S(2)}) copy-start(bf16[256,1024]{1,0:T(8,128)(2,1)} %k.2) | copy-start | bytes 1572868
  0.6 11.0 %copy-start.8 = (f32[8]{0:T(128)S(1)}, f32[8]{0:T(128)}, u32[]{:S(2)}) copy-start(f32[8]{0:T(128)} %rate.7) | copy-start | bytes 100
  0.7 11.0 %copy-start.1 = (bf16[256,1024]{1,0:T(8,128)(2,1)S(1)}, bf16[256,1024]{1,0:T(8,128)(2,1)}, u32[]{:S(2)}) copy-start(bf16[256,1024]{1,0:T(8,128)(2,1)} %v.3) | copy-start | bytes 1572868
  0.7 24.9 %copy-start.6 = (bf16[1,144,3072]{2,1,0:T(8,128)(2,1)S(1)}, bf16[1,144,3072]{2,1,0:T(8,128)(2,1)}, u32[]{:S(2)}) copy-start(bf16[1,144,3072]{2,1,0:T(8,128)(2,1)} %param.23) | copy-start | bytes 2654212
  0.7 11.0 %collective-permute-start.1 = (bf16[144,3072]{1,0:T(8,128)(2,1)}, bf16[144,3072]{1,0:T(8,128)(2,1)S(1)}, u32[]{:S(2)}, u32[]{:S(2)}) collective-permute-start(bf16[144,3072]{1,0:T(8,128)(2,1)} %bitcast.22), channel_id=1, source_target_pairs={{0,4},{4,0},{1,5},{5,1},{2,6},{6,2},{3,7},{7,3},{8,12},{12,8},{9,1... | collective-permute-start | bytes 2654216 | tf_op jit(solution)/shard_map/ppermute | solution.py:398
  0.8 10.9 %collective-permute-start.2 = (bf16[144,3072]{1,0:T(8,128)(2,1)}, bf16[144,3072]{1,0:T(8,128)(2,1)}, u32[]{:S(2)}, u32[]{:S(2)}) collective-permute-start(bf16[144,3072]{1,0:T(8,128)(2,1)} %bitcast.24), channel_id=1, source_target_pairs={{0,4},{4,0},{1,5},{5,1},{2,6},{6,2},{3,7},{7,3},{8,12},{12,8},{9,1... | collective-permute-start | bytes 2654216 | tf_op jit(solution)/shard_map/ppermute | solution.py:398
  5.7 43.6 %collective-permute-start = (bf16[128,3072]{1,0:T(8,128)(2,1)}, bf16[128,3072]{1,0:T(8,128)(2,1)}, u32[]{:S(2)}, u32[]{:S(2)}) collective-permute-start(bf16[128,3072]{1,0:T(8,128)(2,1)} %get-tuple-element.41), channel_id=1, source_target_pairs={{0,1},{1,2},{2,3},{3,0},{4,5},{5,6},{6,7},{7,4},{8,9},{9,10},{10,1... | collective-permute-start | bytes 2359304 | tf_op jit(solution)/shard_map/ppermute | solution.py:398
  7.4 42.0 %collective-permute-start.3 = (bf16[128,3072]{1,0:T(8,128)(2,1)}, bf16[128,3072]{1,0:T(8,128)(2,1)}, u32[]{:S(2)}, u32[]{:S(2)}) collective-permute-start(bf16[128,3072]{1,0:T(8,128)(2,1)} %get-tuple-element.46), channel_id=1, source_target_pairs={{0,2},{1,3},{2,0},{3,1},{4,6},{5,7},{6,4},{7,5},{8,10},{9,11},{10,... | collective-permute-start | bytes 2359304 | tf_op jit(solution)/shard_map/ppermute | solution.py:398
  10.3 39.1 %collective-permute-start.4 = (bf16[128,3072]{1,0:T(8,128)(2,1)}, bf16[128,3072]{1,0:T(8,128)(2,1)}, u32[]{:S(2)}, u32[]{:S(2)}) collective-permute-start(bf16[128,3072]{1,0:T(8,128)(2,1)} %get-tuple-element.47), channel_id=1, source_target_pairs={{0,3},{1,0},{2,1},{3,2},{4,7},{5,4},{6,5},{7,6},{8,11},{9,8},{10,9... | collective-permute-start | bytes 2359304 | tf_op jit(solution)/shard_map/ppermute | solution.py:398
  11.6 13.9 %copy-start.12 = (bf16[144,3072]{1,0:T(8,128)(2,1)}, bf16[144,3072]{1,0:T(8,128)(2,1)S(1)}, u32[]{:S(2)}) copy-start(bf16[144,3072]{1,0:T(8,128)(2,1)S(1)} %collective-permute-done.1.refs_5_) | copy-start | bytes 2654212
  13.6 24.6 %all-to-all-start = ((bf16[64,16,128]{2,1,0:T(8,128)(2,1)}), bf16[64,16,128]{2,1,0:T(8,128)(2,1)S(1)}, u32[]{:S(2)}, u32[]{:S(2)}) async-start(bf16[64,16,128]{2,1,0:T(8,128)(2,1)} %bitcast.5), calls=%async_computation | async-start | bytes 524288 | tf_op jit(solution)/shard_map/all_to_all | solution.py:430
  27.5 10.1 %collective-permute-start.9 = (bf16[144,768]{1,0:T(8,128)(2,1)S(1)}, bf16[144,768]{1,0:T(8,128)(2,1)S(1)}, u32[]{:S(2)}, u32[]{:S(2)}) collective-permute-start(bf16[144,768]{1,0:T(8,128)(2,1)S(1)} %get-tuple-element.57), channel_id=1, source_target_pairs={{0,8},{8,16},{16,24},{24,0},{1,9},{9,17},{17,25},{25,1},{2,10},{10... | collective-permute-start | bytes 663560 | tf_op jit(solution)/shard_map/ppermute | solution.py:398
  27.9 20.8 %collective-permute-start.7 = (bf16[144,768]{1,0:T(8,128)(2,1)}, bf16[144,768]{1,0:T(8,128)(2,1)S(1)}, u32[]{:S(2)}, u32[]{:S(2)}) collective-permute-start(bf16[144,768]{1,0:T(8,128)(2,1)} %get-tuple-element.55), channel_id=1, source_target_pairs={{0,16},{8,24},{16,0},{24,8},{1,17},{9,25},{17,1},{25,9},{2,18},{10... | collective-permute-start | bytes 663560 | tf_op jit(solution)/shard_map/ppermute | solution.py:398
  37.6 11.4 %collective-permute-start.10 = (bf16[144,768]{1,0:T(8,128)(2,1)S(1)}, bf16[144,768]{1,0:T(8,128)(2,1)}, u32[]{:S(2)}, u32[]{:S(2)}) collective-permute-start(bf16[144,768]{1,0:T(8,128)(2,1)S(1)} %get-tuple-element.59), channel_id=1, source_target_pairs={{0,24},{8,0},{16,8},{24,16},{1,25},{9,1},{17,9},{25,17},{2,26},{10... | collective-permute-start | bytes 663560 | tf_op jit(solution)/shard_map/ppermute | solution.py:398
  39.6 36.6 %all-to-all-start.1 = ((bf16[64,16,128]{2,1,0:T(8,128)(2,1)}), bf16[64,16,128]{2,1,0:T(8,128)(2,1)S(1)}, u32[]{:S(2)}, u32[]{:S(2)}) async-start(bf16[64,16,128]{2,1,0:T(8,128)(2,1)} %scan_states.1), calls=%async_computation.1 | async-start | bytes 524288 | tf_op jit(solution)/shard_map/all_to_all | solution.py:457
  48.8 11.4 %copy-start.2 = (bf16[256,1024]{1,0:T(8,128)(2,1)S(1)}, bf16[256,1024]{1,0:T(8,128)(2,1)}, u32[]{:S(2)}) copy-start(bf16[256,1024]{1,0:T(8,128)(2,1)} %q.1) | copy-start | bytes 1572868
  48.8 10.9 %collective-permute-start.8 = (bf16[144,768]{1,0:T(8,128)(2,1)S(1)}, bf16[144,768]{1,0:T(8,128)(2,1)S(1)}, u32[]{:S(2)}, u32[]{:S(2)}) collective-permute-start(bf16[144,768]{1,0:T(8,128)(2,1)S(1)} %get-tuple-element.56.refs_0_), channel_id=1, source_target_pairs={{0,4},{4,0},{1,5},{5,1},{2,6},{6,2},{3,7},{7,3},{8,12},{12,8},{9,1... | collective-permute-start | bytes 663560 | tf_op jit(solution)/shard_map/ppermute | solution.py:398
  49.0 10.6 %collective-permute-start.11 = (bf16[144,768]{1,0:T(8,128)(2,1)S(1)}, bf16[144,768]{1,0:T(8,128)(2,1)S(1)}, u32[]{:S(2)}, u32[]{:S(2)}) collective-permute-start(bf16[144,768]{1,0:T(8,128)(2,1)S(1)} %collective-permute-done.9.refs_2_), channel_id=1, source_target_pairs={{0,4},{4,0},{1,5},{5,1},{2,6},{6,2},{3,7},{7,3},{8,12},{12,8},{9,1... | collective-permute-start | bytes 663560 | tf_op jit(solution)/shard_map/ppermute | solution.py:398
  56.6 17.5 %copy-start.3 = (bf16[288,512]{1,0:T(8,128)(2,1)S(1)}, bf16[288,512]{1,0:T(8,128)(2,1)}, u32[]{:S(2)}) copy-start(bf16[288,512]{1,0:T(8,128)(2,1)} %hidden_part.1.refs_0_) | copy-start | bytes 884740
  56.6 10.1 %collective-permute-start.5 = (bf16[288,512]{1,0:T(8,128)(2,1)}, bf16[288,512]{1,0:T(8,128)(2,1)S(1)}, u32[]{:S(2)}, u32[]{:S(2)}) collective-permute-start(bf16[288,512]{1,0:T(8,128)(2,1)} %hidden_part.1.refs_0_), channel_id=1, source_target_pairs={{0,8},{8,16},{16,24},{24,0},{1,9},{9,17},{17,25},{25,1},{2,10},{10... | collective-permute-start | bytes 884744 | tf_op jit(solution)/shard_map/ppermute | solution.py:398
  57.2 12.3 %collective-permute-start.6 = (bf16[288,512]{1,0:T(8,128)(2,1)}, bf16[288,512]{1,0:T(8,128)(2,1)S(1)}, u32[]{:S(2)}, u32[]{:S(2)}) collective-permute-start(bf16[288,512]{1,0:T(8,128)(2,1)} %hidden_part.1.refs_0_), channel_id=1, source_target_pairs={{0,16},{8,24},{16,0},{24,8},{1,17},{9,25},{17,1},{25,9},{2,18},{10... | collective-permute-start | bytes 884744 | tf_op jit(solution)/shard_map/ppermute | solution.py:398
  59.6 14.5 %collective-permute-start.14 = (bf16[288,512]{1,0:T(8,128)(2,1)}, bf16[288,512]{1,0:T(8,128)(2,1)S(1)}, u32[]{:S(2)}, u32[]{:S(2)}) collective-permute-start(bf16[288,512]{1,0:T(8,128)(2,1)} %hidden_part.1.refs_0_), channel_id=1, source_target_pairs={{0,24},{8,0},{16,8},{24,16},{1,25},{9,1},{17,9},{25,17},{2,26},{10... | collective-permute-start | bytes 884744 | tf_op jit(solution)/shard_map/ppermute | solution.py:398
  59.6 7.1 %collective-permute-start.12 = (bf16[144,768]{1,0:T(8,128)(2,1)S(1)}, bf16[144,768]{1,0:T(8,128)(2,1)S(1)}, u32[]{:S(2)}, u32[]{:S(2)}) collective-permute-start(bf16[144,768]{1,0:T(8,128)(2,1)S(1)} %collective-permute-done.7.refs_4_), channel_id=1, source_target_pairs={{0,4},{4,0},{1,5},{5,1},{2,6},{6,2},{3,7},{7,3},{8,12},{12,8},{9,1... | collective-permute-start | bytes 663560 | tf_op jit(solution)/shard_map/ppermute | solution.py:398
  59.7 7.1 %collective-permute-start.13 = (bf16[144,768]{1,0:T(8,128)(2,1)}, bf16[144,768]{1,0:T(8,128)(2,1)S(1)}, u32[]{:S(2)}, u32[]{:S(2)}) collective-permute-start(bf16[144,768]{1,0:T(8,128)(2,1)} %collective-permute-done.10.refs_6_), channel_id=1, source_target_pairs={{0,4},{4,0},{1,5},{5,1},{2,6},{6,2},{3,7},{7,3},{8,12},{12,8},{9,1... | collective-permute-start | bytes 663560 | tf_op jit(solution)/shard_map/ppermute | solution.py:398
  69.5 27.7 %copy-start.7 = (bf16[256,1024]{1,0:T(8,128)(2,1)S(1)}, bf16[256,1024]{1,0:T(8,128)(2,1)}, u32[]{:S(2)}) copy-start(bf16[256,1024]{1,0:T(8,128)(2,1)} %refs_3_.1) | copy-start | bytes 1572868
  69.5 27.7 %copy-start.9 = (f32[1024]{0:T(1024)S(1)}, f32[1024]{0:T(1024)}, u32[]{:S(2)}) copy-start(f32[1024]{0:T(1024)} %param.17) | copy-start | bytes 12292
  76.2 31.5 %copy-start.10 = (f32[512]{0:T(512)S(1)}, f32[512]{0:T(512)}, u32[]{:S(2)}) copy-start(f32[512]{0:T(512)} %param.20) | copy-start | bytes 6148
  76.2 31.5 %copy-start.11 = (s32[4,1]{0,1:T(1,128)S(1)}, s32[4,1]{0,1:T(1,128)}, u32[]{:S(2)}) copy-start(s32[4,1]{0,1:T(1,128)} %param.19) | copy-start | bytes 52
  76.2 31.5 %all-to-all-start.2 = ((bf16[64,48,128]{2,1,0:T(8,128)(2,1)}), bf16[64,48,128]{2,1,0:T(8,128)(2,1)S(1)}, u32[]{:S(2)}, u32[]{:S(2)}) async-start(bf16[64,48,128]{2,1,0:T(8,128)(2,1)} %bitcast.9), calls=%async_computation.2 | async-start | bytes 1572864 | tf_op jit(solution)/shard_map/all_to_all | solution.py:463
  85.7 1.0 copy-start.4
  97.2 1.2 %copy-start.5 = (f32[256,1024]{1,0:T(8,128)S(1)}, f32[256,1024]{1,0:T(8,128)}, u32[]{:S(2)}) copy-start(f32[256,1024]{1,0:T(8,128)} %copy-done.4) | copy-start | bytes 3145732
where the time goes:
time: 110 us; the launch traced here: 109 us
  starting transfers between devices  43.3 us (39%)
  Pallas kernels  27.6 us (25%)
  waiting for transfers between devices  24.5 us (22%)
  blocking collectives  10.5 us (10%)
  local copies, waits for them, and re-layouts  2.26 us (2%)
    ppermute x15, waiting for transfers between devices, shift(): return lax.ppermute(array, axis, [(i, (i + by) % n) for i in range(n)])  16.4 us
    ppermute x15, starting transfers between devices, shift(): return lax.ppermute(array, axis, [(i, (i + by) % n) for i in range(n)])  14.1 us
    all_to_all x1, starting transfers between devices, on_device(): pieces = lax.all_to_all(pieces, CTX, 0, 0, tiled=True)  12 us
    psum x1, blocking collectives, on_device(): squares = [lax.psum(squares, 'exp')]  10.5 us
    all_to_all x1, starting transfers between devices, on_device(): prefix = lax.all_to_all(pieces, CTX, 0, 0, tiled=True).reshape(width, HEAD)  9.13 us
    all_to_all x1, waiting for transfers between devices, on_device(): parts = lax.all_to_all(parts, ('z', 'core', 'exp'), 0, 0, tiled=True)  8.13 us
    all_to_all x1, starting transfers between devices, on_device(): parts = lax.all_to_all(parts, ('z', 'core', 'exp'), 0, 0, tiled=True)  8.1 us
    pallas_call x1, Pallas kernels, hidden_part(): pl.pallas_call(functools.partial(_hidden_kernel, count), in_specs=[pl.Blo...  7.23 us
  transfers between devices with their start and end apart: 18, of which 4 were waited for; matrix products, arithmetic and copies ran while one was open for 0% of the time, Pallas kernels for 24%

commit v1 on v0

--- a/solution.py
+++ b/solution.py
@@ -224,49 +224,75 @@
     )(ids, rows)
 
 
-def _hidden_kernel(count, *refs):
-    sources, out = refs[: count + 4], refs[count + 4]
-    rows, weights, sems = refs[count + 5 :]
-    units = weights.shape[0] // 4
-    targets = [rows.at[i * TILE : (i + 1) * TILE, :] for i in range(count)]
-    targets += [weights.at[i * units : (i + 1) * units, :] for i in range(4)]
-    copies = [
-        pltpu.make_async_copy(source, target, sems.at[i])
-        for i, (source, target) in enumerate(zip(sources, targets))
-    ]
-    order = list(range(count, count + 4)) + list(range(count))
-    for i in order:
-        copies[i].start()
-    for i in range(4):
+def _turn_kernel(gate_own, gate_other, up_own, up_other, out, held):
+    units, half = gate_own.shape[0], held.shape[0] // 2
+    held[...] = jnp.zeros_like(held)
+    for i, part in enumerate((gate_own, gate_other)):
+        held[i * units : (i + 1) * units, :] = part[...]
+    for i, part in enumerate((up_own, up_other)):
+        at = half + i * units
+        held[at : at + units, :] = part[...]
+    out[...] = jnp.transpose(held[...])
+
+
+def turn_weights(weights):
+    units, model = weights[0].shape
+    half = -(-2 * units // HEAD) * HEAD
+    step = 512
+    return pl.pallas_call(
+        _turn_kernel,
+        grid=(model // step,),
+        in_specs=[pl.BlockSpec((units, step), lambda i: (0, i))] * 4,
+        out_specs=pl.BlockSpec((step, 2 * half), lambda i: (i, 0)),
+        out_shape=jax.ShapeDtypeStruct((model, 2 * half), BF),
+        scratch_shapes=[pltpu.VMEM((2 * half, step), BF)],
+        compiler_params=pltpu.CompilerParams(vmem_limit_bytes=58 << 20),
+        name="turn_weights",
+    )(*weights)
+
+
+def _hidden_kernel(count, cuts, *refs):
+    sources, weight, out, rows, held, sems = refs[:count], *refs[count:]
+    deep = held.shape[0] // cuts
+    copies = []
+    for i, source in enumerate(sources):
+        target = rows.at[i * TILE : (i + 1) * TILE, :]
+        copies.append(pltpu.make_async_copy(source, target, sems.at[i]))
+    for i in range(cuts):
+        at = slice(i * deep, (i + 1) * deep)
+        copies.append(
+            pltpu.make_async_copy(weight.at[at, :], held.at[at, :], sems.at[count + i])
+        )
+    for copy in copies:
+        copy.start()
+    for copy in copies[:count]:
+        copy.wait()
+    both = None
+    for i in range(cuts):
         copies[count + i].wait()
-    dims = (((1,), (1,)), ((), ()))
-    wide = 2 * TILE
-    for j in range(count // 2):
-        copies[2 * j].wait()
-        copies[2 * j + 1].wait()
-        at = slice(j * wide, (j + 1) * wide)
-        both = lax.dot_general(
-            weights[...], rows[at, :], dims, preferred_element_type=F32
-        )
-        gate, up = both[: 2 * units], both[2 * units :]
-        out[:, at] = (jax.nn.silu(gate) * up).astype(BF)
-
-
-def hidden_part(rows, weights):
-    count, (units, model) = len(rows), weights[0].shape
-    return pl.pallas_call(
-        functools.partial(_hidden_kernel, count),
-        in_specs=[pl.BlockSpec(memory_space=pl.ANY)] * (count + 4),
+        at = slice(i * deep, (i + 1) * deep)
+        term = jnp.dot(rows[:, at], held[at, :], preferred_element_type=F32)
+        both = term if both is None else both + term
+    half, units = held.shape[1] // 2, out.shape[0]
+    value = (jax.nn.silu(both[:, :half]) * both[:, half:]).astype(BF)
+    out[...] = jnp.transpose(value)[:units]
+
+
+def hidden_part(rows, weight, units):
+    count, (model, wide), cuts = len(rows), weight.shape, 4
+    return pl.pallas_call(
+        functools.partial(_hidden_kernel, count, cuts),
+        in_specs=[pl.BlockSpec(memory_space=pl.ANY)] * (count + 1),
         out_specs=pl.BlockSpec(memory_space=pltpu.VMEM),
-        out_shape=jax.ShapeDtypeStruct((2 * units, count * TILE), BF),
+        out_shape=jax.ShapeDtypeStruct((units, count * TILE), BF),
         scratch_shapes=[
             pltpu.VMEM((count * TILE, model), BF),
-            pltpu.VMEM((4 * units, model), BF),
-            pltpu.SemaphoreType.DMA((count + 4,)),
+            pltpu.VMEM((model, wide), BF),
+            pltpu.SemaphoreType.DMA((count + cuts,)),
         ],
         compiler_params=pltpu.CompilerParams(vmem_limit_bytes=58 << 20),
         name="hidden_part",
-    )(*rows, *weights)
+    )(*rows, weight)
 
 
 def _split_kernel(n_z, weight, *outs):
@@ -428,8 +454,12 @@
     states, w_down = lax.optimization_barrier((states, w_down))
     pieces = states.reshape(n_ctx, width // n_ctx, HEAD)
     pieces = lax.all_to_all(pieces, CTX, 0, 0, tiled=True)
+    chunks = list(split_columns(w_down[0], n_z, n_x))
+    gate_other, _ = lax.optimization_barrier((gate_other, chunks[0]))
+    turned = turn_weights((gate_own, gate_other, up_own, up_other))
+    chunks[3], _ = lax.optimization_barrier((chunks[3], turned))
+    pieces, _ = lax.optimization_barrier((pieces, turned))
     pieces = scan_states(float(tokens), decay_rate, pieces)
-    chunks = list(split_columns(w_down[0], n_z, n_x))
     down_own, down_other = [chunks[0]] + [None] * (n_x - 1), [None] * n_x
     lanes = (
         (("x", 1), ("x", 3), ("core", 1), ("core", 3)),
@@ -448,8 +478,7 @@
                 down_other[k] = last
     arrived[LAST], _ = lax.optimization_barrier((arrived[LAST], pieces))
 
-    weights = (gate_own, gate_other, up_own, up_other)
-    hidden = hidden_part(arrived, weights)
+    hidden = hidden_part(arrived, turned, 2 * units)
     hidden, queries = lax.optimization_barrier((hidden, queries))
     hidden = [hidden] + [shift(hidden, "x", k) for k in range(1, n_x)]
     intra = intra_part(decay_rate, queries, keys, values)

time: 110 us -> 111 us (level)
  waiting for transfers between devices: 24.5 us -> 18 us
  Pallas kernels: 27.6 us -> 33.7 us
  starting transfers between devices: 43.3 us -> 44.8 us
    ppermute x15, waiting for transfers between devices: 16.4 us -> 9.9 us  [shift(): return lax.ppermute(array, axis, [(i, (i + by) % n) for i in range(n)])]
    pallas_call x1 -> x2, Pallas kernels: 7.23 us -> 13.4 us  [the longest x1 6.91 us: hidden_part(): pl.pallas_call(functools.partial(_hidden_kernel, count, cuts), in_specs=[...]
    all_to_all x1, starting transfers between devices: 9.13 us -> 10.6 us  [on_device(): prefix = lax.all_to_all(pieces, CTX, 0, 0, tiled=True).reshape(width, HEAD)]
  transfers between devices with their start and end apart: 18 -> 18, of which waited for: 4 -> 4; matrix products, arithmetic and copies ran while one was open for 0% -> 0% of each run, Pallas kernels for 24% -> 29%
where the time goes in v1:
time: 111 us; the launch traced here: 110 us
  starting transfers between devices  44.8 us (40%)
  Pallas kernels  33.7 us (30%)
  waiting for transfers between devices  18 us (16%)
  blocking collectives  10.5 us (9%)
  local copies, waits for them, and re-layouts  2.26 us (2%)
    ppermute x15, starting transfers between devices, shift(): return lax.ppermute(array, axis, [(i, (i + by) % n) for i in range(n)])  14.1 us
    all_to_all x1, starting transfers between devices, on_device(): pieces = lax.all_to_all(pieces, CTX, 0, 0, tiled=True)  12 us
    all_to_all x1, starting transfers between devices, on_device(): prefix = lax.all_to_all(pieces, CTX, 0, 0, tiled=True).reshape(width, HEAD)  10.6 us
    psum x1, blocking collectives, on_device(): squares = [lax.psum(squares, 'exp')]  10.5 us
    ppermute x15, waiting for transfers between devices, shift(): return lax.ppermute(array, axis, [(i, (i + by) % n) for i in range(n)])  9.9 us
    all_to_all x1, waiting for transfers between devices, on_device(): parts = lax.all_to_all(parts, ('z', 'core', 'exp'), 0, 0, tiled=True)  8.11 us
    all_to_all x1, starting transfers between devices, on_device(): parts = lax.all_to_all(parts, ('z', 'core', 'exp'), 0, 0, tiled=True)  8.07 us
    pallas_call x1, Pallas kernels, hidden_part(): pl.pallas_call(functools.partial(_hidden_kernel, count, cuts), in_specs=[...  6.91 us
  transfers between devices with their start and end apart: 18, of which 4 were waited for; matrix products, arithmetic and copies ran while one was open for 0% of the time, Pallas kernels for 29%

profile of v1, /device:TPU:6, one launch (start us, length us, event | category | flops | bytes accessed | tf_op | source)
XLA Modules:
  0.0 110.1 jit_solution(6012119189801995918)
XLA Ops:
  0.8 0.5 collective-permute-start.2
  1.3 4.3 %pick_tiles.1 = (bf16[128,3072]{1,0:T(8,128)(2,1)}, bf16[128,3072]{1,0:T(8,128)(2,1)}, bf16[128,3072]{1,0:T(8,128)(2,1)}, bf16[128,3072]{1,0:T(8,128)(2,1)}) custom-call(s32[4]{0:T(128)} %bitcast.20, bf16[512,3072]{1,0:T(8,128)(2,1)} %rows.1), custom_call_target="tpu_custom_call" | custom-call | tf_op jit(solution)/shard_map/pick_tiles/pallas_call | solution.py:209
  5.6 1.6 %collective-permute-start = (bf16[128,3072]{1,0:T(8,128)(2,1)}, bf16[128,3072]{1,0:T(8,128)(2,1)}, u32[]{:S(2)}, u32[]{:S(2)}) collective-permute-start(bf16[128,3072]{1,0:T(8,128)(2,1)} %get-tuple-element.44), channel_id=1, source_target_pairs={{0,1},{1,2},{2,3},{3,0},{4,5},{5,6},{6,7},{7,4},{8,9},{9,10},{10,1... | collective-permute-start | bytes 2359304 | tf_op jit(solution)/shard_map/ppermute | solution.py:424
  7.3 2.9 %collective-permute-start.3 = (bf16[128,3072]{1,0:T(8,128)(2,1)}, bf16[128,3072]{1,0:T(8,128)(2,1)}, u32[]{:S(2)}, u32[]{:S(2)}) collective-permute-start(bf16[128,3072]{1,0:T(8,128)(2,1)} %get-tuple-element.55), channel_id=1, source_target_pairs={{0,2},{1,3},{2,0},{3,1},{4,6},{5,7},{6,4},{7,5},{8,10},{9,11},{10,... | collective-permute-start | bytes 2359304 | tf_op jit(solution)/shard_map/ppermute | solution.py:424
  10.2 1.3 %collective-permute-start.4 = (bf16[128,3072]{1,0:T(8,128)(2,1)}, bf16[128,3072]{1,0:T(8,128)(2,1)}, u32[]{:S(2)}, u32[]{:S(2)}) collective-permute-start(bf16[128,3072]{1,0:T(8,128)(2,1)} %get-tuple-element.56), channel_id=1, source_target_pairs={{0,3},{1,0},{2,1},{3,2},{4,7},{5,4},{6,5},{7,6},{8,11},{9,8},{10,9... | collective-permute-start | bytes 2359304 | tf_op jit(solution)/shard_map/ppermute | solution.py:424
  11.5 1.9 %local_states.1 = bf16[1024,128]{1,0:T(8,128)(2,1)} custom-call(f32[8]{0:T(128)S(1)} %copy-done.8, bf16[256,1024]{1,0:T(8,128)(2,1)S(1)} %copy-done, bf16[256,1024]{1,0:T(8,128)(2,1)S(1)} %copy-done.1), custom_call_target="tpu_custom_call" | custom-call | tf_op jit(solution)/shard_map/local_states/pallas_call | solution.py:36
  13.5 12.0 %all-to-all-start = ((bf16[64,16,128]{2,1,0:T(8,128)(2,1)}), bf16[64,16,128]{2,1,0:T(8,128)(2,1)S(1)}, u32[]{:S(2)}, u32[]{:S(2)}) async-start(bf16[64,16,128]{2,1,0:T(8,128)(2,1)} %bitcast.5), calls=%async_computation | async-start | bytes 524288 | tf_op jit(solution)/shard_map/all_to_all | solution.py:456
  25.4 1.9 %split_columns.1 = (bf16[144,768]{1,0:T(8,128)(2,1)S(1)}, bf16[144,768]{1,0:T(8,128)(2,1)S(1)}, bf16[144,768]{1,0:T(8,128)(2,1)}, bf16[144,768]{1,0:T(8,128)(2,1)S(1)}) custom-call(bf16[144,3072]{1,0:T(8,128)(2,1)S(1)} %bitcast.17), custom_call_target="tpu_custom_call" | custom-call | tf_op jit(solution)/shard_map/split_columns/pallas_call | solution.py:321
  27.3 0.5 collective-permute-start.9
  27.8 2.5 %collective-permute-start.7 = (bf16[144,768]{1,0:T(8,128)(2,1)}, bf16[144,768]{1,0:T(8,128)(2,1)S(1)}, u32[]{:S(2)}, u32[]{:S(2)}) collective-permute-start(bf16[144,768]{1,0:T(8,128)(2,1)} %get-tuple-element.60), channel_id=1, source_target_pairs={{0,16},{8,24},{16,0},{24,8},{1,17},{9,25},{17,1},{25,9},{2,18},{10... | collective-permute-start | bytes 663560 | tf_op jit(solution)/shard_map/ppermute | solution.py:424
  30.3 6.5 %turn_weights.1.refs_4_ = bf16[3072,768]{1,0:T(8,128)(2,1)} custom-call(bf16[144,3072]{1,0:T(8,128)(2,1)} %bitcast.23, bf16[144,3072]{1,0:T(8,128)(2,1)} %copy-done.12, bf16[144,3072]{1,0:T(8,128)(2,1)} %bitcast.25, bf16[144,3072]{1,0:T(8,128)(2,1)} %collective-permute-done.2.up_other), custom_call_target="tpu_custom_call" | custom-call | tf_op jit(solution)/shard_map/turn_weights/pallas_call | solution.py:242
  36.8 0.6 collective-permute-done.9.refs_2_
  37.4 0.6 collective-permute-start.10
  38.0 1.4 %scan_states.1 = bf16[64,16,128]{2,1,0:T(8,128)(2,1)} custom-call(f32[8]{0:T(128)S(1)} %copy-done.8, bf16[64,16,128]{2,1,0:T(8,128)(2,1)S(1)} %all-to-all-done.states), custom_call_target="tpu_custom_call" | custom-call | tf_op jit(solution)/shard_map/scan_states/pallas_call | solution.py:58
  39.5 10.6 %all-to-all-start.1 = ((bf16[64,16,128]{2,1,0:T(8,128)(2,1)}), bf16[64,16,128]{2,1,0:T(8,128)(2,1)S(1)}, u32[]{:S(2)}, u32[]{:S(2)}) async-start(bf16[64,16,128]{2,1,0:T(8,128)(2,1)} %scan_states.1), calls=%async_computation.1 | async-start | bytes 524288 | tf_op jit(solution)/shard_map/all_to_all | solution.py:486
  50.7 6.9 %hidden_part.1.refs_0_ = bf16[288,512]{1,0:T(8,128)(2,1)} custom-call(bf16[128,3072]{1,0:T(8,128)(2,1)} %get-tuple-element.43.refs_0_, bf16[128,3072]{1,0:T(8,128)(2,1)} %collective-permute-done.refs_1_, bf16[128,3072]{1,0:T(8,128)(2,1)} %collective-permute-done.3.refs_2_, bf16[128,3072]{1,0:T(8,128)(2,1)} %collective-permute-done.4.refs_3_, ...), custom_call_target="tpu_custom_call" | custom-call | tf_op jit(solution)/shard_map/hidden_part/pallas_call | solution.py:283
  57.7 0.5 collective-permute-start.5
  58.2 2.5 %collective-permute-start.6 = (bf16[288,512]{1,0:T(8,128)(2,1)}, bf16[288,512]{1,0:T(8,128)(2,1)S(1)}, u32[]{:S(2)}, u32[]{:S(2)}) collective-permute-start(bf16[288,512]{1,0:T(8,128)(2,1)} %hidden_part.1.refs_0_), channel_id=1, source_target_pairs={{0,16},{8,24},{16,0},{24,8},{1,17},{9,25},{17,1},{25,9},{2,18},{10... | collective-permute-start | bytes 884744 | tf_op jit(solution)/shard_map/ppermute | solution.py:424
  60.7 0.5 collective-permute-start.13
  61.2 2.0 %intra_part.1.intra = f32[256,1024]{1,0:T(8,128)S(1)} custom-call(f32[8]{0:T(128)S(1)} %copy-done.8, bf16[256,1024]{1,0:T(8,128)(2,1)S(1)} %copy-done.2, bf16[256,1024]{1,0:T(8,128)(2,1)S(1)} %copy-done, bf16[256,1024]{1,0:T(8,128)(2,1)S(1)} %copy-done.1), custom_call_target="tpu_custom_call" | custom-call | tf_op jit(solution)/shard_map/intra_part/pallas_call | solution.py:92
  63.2 4.6 %collective-permute-done.5.refs_1_ = bf16[288,512]{1,0:T(8,128)(2,1)S(1)} collective-permute-done((bf16[288,512]{1,0:T(8,128)(2,1)}, bf16[288,512]{1,0:T(8,128)(2,1)S(1)}, u32[]{:S(2)}, u32[]{:S(2)}) %collective-permute-start.5) | collective-permute-done | bytes 294944 | tf_op jit(solution)/shard_map/ppermute | solution.py:424
  67.8 2.7 %stack_rows.1.weight = bf16[1152,768]{1,0:T(8,128)(2,1)S(1)} custom-call(bf16[144,768]{1,0:T(8,128)(2,1)S(1)} %get-tuple-element.61.refs_0_, bf16[144,768]{1,0:T(8,128)(2,1)S(1)} %collective-permute-done.8.refs_1_, bf16[144,768]{1,0:T(8,128)(2,1)S(1)} %collective-permute-done.9.refs_2_, bf16[144,768]{1,0:T(8,128)(2,1)S(1)} %collective-permute-done.11.refs_3_, ...), custom_call_target="tpu_custom_call" | custom-call | tf_op jit(solution)/shard_map/stack_rows/pallas_call | solution.py:346
  70.6 4.7 %collective-permute-done.14.refs_3_ = bf16[288,512]{1,0:T(8,128)(2,1)S(1)} collective-permute-done((bf16[288,512]{1,0:T(8,128)(2,1)}, bf16[288,512]{1,0:T(8,128)(2,1)S(1)}, u32[]{:S(2)}, u32[]{:S(2)}) %collective-permute-start.14) | collective-permute-done | bytes 294944 | tf_op jit(solution)/shard_map/ppermute | solution.py:424
  75.2 2.1 %down_part.1 = bf16[16,4,48,128]{3,2,1,0:T(8,128)(2,1)} custom-call(bf16[1152,768]{1,0:T(8,128)(2,1)S(1)} %stack_rows.1.weight, bf16[288,512]{1,0:T(8,128)(2,1)S(1)} %copy-done.3, bf16[288,512]{1,0:T(8,128)(2,1)S(1)} %collective-permute-done.5.refs_1_, bf16[288,512]{1,0:T(8,128)(2,1)S(1)} %collective-permute-done.6.refs_2_, ...), custom_call_target="tpu_custom_call" | custom-call | tf_op jit(solution)/shard_map/down_part/pallas_call | solution.py:376
  77.3 8.1 %all-to-all-start.2 = ((bf16[64,48,128]{2,1,0:T(8,128)(2,1)}), bf16[64,48,128]{2,1,0:T(8,128)(2,1)S(1)}, u32[]{:S(2)}, u32[]{:S(2)}) async-start(bf16[64,48,128]{2,1,0:T(8,128)(2,1)} %bitcast.11), calls=%async_computation.2 | async-start | bytes 1572864 | tf_op jit(solution)/shard_map/all_to_all | solution.py:492
  85.4 1.3 %mix_part.1 = (f32[256,1024]{1,0:T(8,128)S(1)}, f32[1,256]{1,0:T(1,128)S(1)}) custom-call(f32[8]{0:T(128)S(1)} %copy-done.8, f32[256,1024]{1,0:T(8,128)S(1)} %intra_part.1.intra, bf16[256,1024]{1,0:T(8,128)(2,1)S(1)} %copy-done.2, bf16[1024,128]{1,0:T(8,128)(2,1)S(1)} %bitcast.16), custom_call_target="tpu_custom_call" | custom-call | tf_op jit(solution)/shard_map/mix_part/pallas_call | solution.py:126
  86.8 1.0 copy-done.4
  87.7 10.5 %psum.7.refs_0_ = f32[1,256]{1,0:T(1,128)S(1)} all-reduce(f32[1,256]{1,0:T(1,128)S(1)} %get-tuple-element.73), channel_id=1, replica_groups=mesh['z'=8,'x'=4,'core'=2,'exp'=4] {'exp'}, use_global_device_ids=true, to_apply=%region_0.0 | all-reduce | flops 256 | bytes 2048 | tf_op jit(solution)/shard_map/psum | solution.py:496
  98.3 1.2 %copy-done.5 = f32[256,1024]{1,0:T(8,128)S(1)} copy-done((f32[256,1024]{1,0:T(8,128)S(1)}, f32[256,1024]{1,0:T(8,128)}, u32[]{:S(2)}) %copy-start.5) | copy-done | bytes 1048600
  99.5 1.2 %norm_part.1 = bf16[256,1024]{1,0:T(8,128)(2,1)} custom-call(f32[1,256]{1,0:T(1,128)S(1)} %psum.7.refs_0_, f32[256,1024]{1,0:T(8,128)S(1)} %copy-done.5, f32[1,1024]{1,0:T(1,128)S(1)} %bitcast.18, bf16[256,1024]{1,0:T(8,128)(2,1)S(1)} %copy-done.7), custom_call_target="tpu_custom_call" | custom-call | tf_op jit(solution)/shard_map/norm_part/pallas_call | solution.py:161
  100.7 8.1 %all-to-all-done.2 = bf16[64,48,128]{2,1,0:T(8,128)(2,1)S(1)} async-done(((bf16[64,48,128]{2,1,0:T(8,128)(2,1)}), bf16[64,48,128]{2,1,0:T(8,128)(2,1)S(1)}, u32[]{:S(2)}, u32[]{:S(2)}) %all-to-all-start.2) | async-done | bytes 786464 | tf_op jit(solution)/shard_map/all_to_all | solution.py:492
  108.8 1.3 %finish_part.1 = bf16[48,512]{1,0:T(8,128)(2,1)} custom-call(s32[4]{0:T(128)S(1)} %bitcast.21, bf16[8,2,4,48,128]{4,3,2,1,0:T(8,128)(2,1)S(1)} %bitcast.15, f32[1,512]{1,0:T(1,128)S(1)} %bitcast.19), custom_call_target="tpu_custom_call" | custom-call | tf_op jit(solution)/shard_map/finish_part/pallas_call | solution.py:412
  (43 shorter events, 0.8 us)
Async XLA Ops:
  0.6 10.9 %copy-start = (bf16[256,1024]{1,0:T(8,128)(2,1)S(1)}, bf16[256,1024]{1,0:T(8,128)(2,1)}, u32[]{:S(2)}) copy-start(bf16[256,1024]{1,0:T(8,128)(2,1)} %k.2) | copy-start | bytes 1572868
  0.6 10.9 %copy-start.8 = (f32[8]{0:T(128)S(1)}, f32[8]{0:T(128)}, u32[]{:S(2)}) copy-start(f32[8]{0:T(128)} %rate.7) | copy-start | bytes 100
  0.7 10.9 %copy-start.1 = (bf16[256,1024]{1,0:T(8,128)(2,1)S(1)}, bf16[256,1024]{1,0:T(8,128)(2,1)}, u32[]{:S(2)}) copy-start(bf16[256,1024]{1,0:T(8,128)(2,1)} %v.3) | copy-start | bytes 1572868
  0.7 24.8 %copy-start.6 = (bf16[1,144,3072]{2,1,0:T(8,128)(2,1)S(1)}, bf16[1,144,3072]{2,1,0:T(8,128)(2,1)}, u32[]{:S(2)}) copy-start(bf16[1,144,3072]{2,1,0:T(8,128)(2,1)} %param.23) | copy-start | bytes 2654212
  0.7 10.8 %collective-permute-start.1 = (bf16[144,3072]{1,0:T(8,128)(2,1)}, bf16[144,3072]{1,0:T(8,128)(2,1)S(1)}, u32[]{:S(2)}, u32[]{:S(2)}) collective-permute-start(bf16[144,3072]{1,0:T(8,128)(2,1)} %bitcast.22), channel_id=1, source_target_pairs={{0,4},{4,0},{1,5},{5,1},{2,6},{6,2},{3,7},{7,3},{8,12},{12,8},{9,1... | collective-permute-start | bytes 2654216 | tf_op jit(solution)/shard_map/ppermute | solution.py:424
  0.8 10.7 %collective-permute-start.2 = (bf16[144,3072]{1,0:T(8,128)(2,1)}, bf16[144,3072]{1,0:T(8,128)(2,1)}, u32[]{:S(2)}, u32[]{:S(2)}) collective-permute-start(bf16[144,3072]{1,0:T(8,128)(2,1)} %bitcast.24), channel_id=1, source_target_pairs={{0,4},{4,0},{1,5},{5,1},{2,6},{6,2},{3,7},{7,3},{8,12},{12,8},{9,1... | collective-permute-start | bytes 2654216 | tf_op jit(solution)/shard_map/ppermute | solution.py:424
  5.6 45.1 %collective-permute-start = (bf16[128,3072]{1,0:T(8,128)(2,1)}, bf16[128,3072]{1,0:T(8,128)(2,1)}, u32[]{:S(2)}, u32[]{:S(2)}) collective-permute-start(bf16[128,3072]{1,0:T(8,128)(2,1)} %get-tuple-element.44), channel_id=1, source_target_pairs={{0,1},{1,2},{2,3},{3,0},{4,5},{5,6},{6,7},{7,4},{8,9},{9,10},{10,1... | collective-permute-start | bytes 2359304 | tf_op jit(solution)/shard_map/ppermute | solution.py:424
  7.3 43.5 %collective-permute-start.3 = (bf16[128,3072]{1,0:T(8,128)(2,1)}, bf16[128,3072]{1,0:T(8,128)(2,1)}, u32[]{:S(2)}, u32[]{:S(2)}) collective-permute-start(bf16[128,3072]{1,0:T(8,128)(2,1)} %get-tuple-element.55), channel_id=1, source_target_pairs={{0,2},{1,3},{2,0},{3,1},{4,6},{5,7},{6,4},{7,5},{8,10},{9,11},{10,... | collective-permute-start | bytes 2359304 | tf_op jit(solution)/shard_map/ppermute | solution.py:424
  10.2 40.6 %collective-permute-start.4 = (bf16[128,3072]{1,0:T(8,128)(2,1)}, bf16[128,3072]{1,0:T(8,128)(2,1)}, u32[]{:S(2)}, u32[]{:S(2)}) collective-permute-start(bf16[128,3072]{1,0:T(8,128)(2,1)} %get-tuple-element.56), channel_id=1, source_target_pairs={{0,3},{1,0},{2,1},{3,2},{4,7},{5,4},{6,5},{7,6},{8,11},{9,8},{10,9... | collective-permute-start | bytes 2359304 | tf_op jit(solution)/shard_map/ppermute | solution.py:424
  11.5 13.9 %copy-start.12 = (bf16[144,3072]{1,0:T(8,128)(2,1)}, bf16[144,3072]{1,0:T(8,128)(2,1)S(1)}, u32[]{:S(2)}) copy-start(bf16[144,3072]{1,0:T(8,128)(2,1)S(1)} %collective-permute-done.1.gate_other) | copy-start | bytes 2654212
  13.5 24.6 %all-to-all-start = ((bf16[64,16,128]{2,1,0:T(8,128)(2,1)}), bf16[64,16,128]{2,1,0:T(8,128)(2,1)S(1)}, u32[]{:S(2)}, u32[]{:S(2)}) async-start(bf16[64,16,128]{2,1,0:T(8,128)(2,1)} %bitcast.5), calls=%async_computation | async-start | bytes 524288 | tf_op jit(solution)/shard_map/all_to_all | solution.py:456
  27.3 10.1 %collective-permute-start.9 = (bf16[144,768]{1,0:T(8,128)(2,1)S(1)}, bf16[144,768]{1,0:T(8,128)(2,1)S(1)}, u32[]{:S(2)}, u32[]{:S(2)}) collective-permute-start(bf16[144,768]{1,0:T(8,128)(2,1)S(1)} %get-tuple-element.62), channel_id=1, source_target_pairs={{0,8},{8,16},{16,24},{24,0},{1,9},{9,17},{17,25},{25,1},{2,10},{10... | collective-permute-start | bytes 663560 | tf_op jit(solution)/shard_map/ppermute | solution.py:424
  27.8 22.3 %collective-permute-start.7 = (bf16[144,768]{1,0:T(8,128)(2,1)}, bf16[144,768]{1,0:T(8,128)(2,1)S(1)}, u32[]{:S(2)}, u32[]{:S(2)}) collective-permute-start(bf16[144,768]{1,0:T(8,128)(2,1)} %get-tuple-element.60), channel_id=1, source_target_pairs={{0,16},{8,24},{16,0},{24,8},{1,17},{9,25},{17,1},{25,9},{2,18},{10... | collective-permute-start | bytes 663560 | tf_op jit(solution)/shard_map/ppermute | solution.py:424
  37.4 12.9 %collective-permute-start.10 = (bf16[144,768]{1,0:T(8,128)(2,1)S(1)}, bf16[144,768]{1,0:T(8,128)(2,1)}, u32[]{:S(2)}, u32[]{:S(2)}) collective-permute-start(bf16[144,768]{1,0:T(8,128)(2,1)S(1)} %get-tuple-element.65), channel_id=1, source_target_pairs={{0,24},{8,0},{16,8},{24,16},{1,25},{9,1},{17,9},{25,17},{2,26},{10... | collective-permute-start | bytes 663560 | tf_op jit(solution)/shard_map/ppermute | solution.py:424
  39.5 37.9 %all-to-all-start.1 = ((bf16[64,16,128]{2,1,0:T(8,128)(2,1)}), bf16[64,16,128]{2,1,0:T(8,128)(2,1)S(1)}, u32[]{:S(2)}, u32[]{:S(2)}) async-start(bf16[64,16,128]{2,1,0:T(8,128)(2,1)} %scan_states.1), calls=%async_computation.1 | async-start | bytes 524288 | tf_op jit(solution)/shard_map/all_to_all | solution.py:486
  50.1 11.1 %copy-start.2 = (bf16[256,1024]{1,0:T(8,128)(2,1)S(1)}, bf16[256,1024]{1,0:T(8,128)(2,1)}, u32[]{:S(2)}) copy-start(bf16[256,1024]{1,0:T(8,128)(2,1)} %q.1) | copy-start | bytes 1572868
  50.1 10.6 %collective-permute-start.8 = (bf16[144,768]{1,0:T(8,128)(2,1)S(1)}, bf16[144,768]{1,0:T(8,128)(2,1)S(1)}, u32[]{:S(2)}, u32[]{:S(2)}) collective-permute-start(bf16[144,768]{1,0:T(8,128)(2,1)S(1)} %get-tuple-element.61.refs_0_), channel_id=1, source_target_pairs={{0,4},{4,0},{1,5},{5,1},{2,6},{6,2},{3,7},{7,3},{8,12},{12,8},{9,1... | collective-permute-start | bytes 663560 | tf_op jit(solution)/shard_map/ppermute | solution.py:424
  50.4 10.3 %collective-permute-start.11 = (bf16[144,768]{1,0:T(8,128)(2,1)S(1)}, bf16[144,768]{1,0:T(8,128)(2,1)S(1)}, u32[]{:S(2)}, u32[]{:S(2)}) collective-permute-start(bf16[144,768]{1,0:T(8,128)(2,1)S(1)} %collective-permute-done.9.refs_2_), channel_id=1, source_target_pairs={{0,4},{4,0},{1,5},{5,1},{2,6},{6,2},{3,7},{7,3},{8,12},{12,8},{9,1... | collective-permute-start | bytes 663560 | tf_op jit(solution)/shard_map/ppermute | solution.py:424
  57.7 17.5 %copy-start.3 = (bf16[288,512]{1,0:T(8,128)(2,1)S(1)}, bf16[288,512]{1,0:T(8,128)(2,1)}, u32[]{:S(2)}) copy-start(bf16[288,512]{1,0:T(8,128)(2,1)} %hidden_part.1.refs_0_) | copy-start | bytes 884740
  57.7 10.1 %collective-permute-start.5 = (bf16[288,512]{1,0:T(8,128)(2,1)}, bf16[288,512]{1,0:T(8,128)(2,1)S(1)}, u32[]{:S(2)}, u32[]{:S(2)}) collective-permute-start(bf16[288,512]{1,0:T(8,128)(2,1)} %hidden_part.1.refs_0_), channel_id=1, source_target_pairs={{0,8},{8,16},{16,24},{24,0},{1,9},{9,17},{17,25},{25,1},{2,10},{10... | collective-permute-start | bytes 884744 | tf_op jit(solution)/shard_map/ppermute | solution.py:424
  58.2 12.3 %collective-permute-start.6 = (bf16[288,512]{1,0:T(8,128)(2,1)}, bf16[288,512]{1,0:T(8,128)(2,1)S(1)}, u32[]{:S(2)}, u32[]{:S(2)}) collective-permute-start(bf16[288,512]{1,0:T(8,128)(2,1)} %hidden_part.1.refs_0_), channel_id=1, source_target_pairs={{0,16},{8,24},{16,0},{24,8},{1,17},{9,25},{17,1},{25,9},{2,18},{10... | collective-permute-start | bytes 884744 | tf_op jit(solution)/shard_map/ppermute | solution.py:424
  60.7 14.5 %collective-permute-start.14 = (bf16[288,512]{1,0:T(8,128)(2,1)}, bf16[288,512]{1,0:T(8,128)(2,1)S(1)}, u32[]{:S(2)}, u32[]{:S(2)}) collective-permute-start(bf16[288,512]{1,0:T(8,128)(2,1)} %hidden_part.1.refs_0_), channel_id=1, source_target_pairs={{0,24},{8,0},{16,8},{24,16},{1,25},{9,1},{17,9},{25,17},{2,26},{10... | collective-permute-start | bytes 884744 | tf_op jit(solution)/shard_map/ppermute | solution.py:424
  60.7 7.1 %collective-permute-start.12 = (bf16[144,768]{1,0:T(8,128)(2,1)S(1)}, bf16[144,768]{1,0:T(8,128)(2,1)S(1)}, u32[]{:S(2)}, u32[]{:S(2)}) collective-permute-start(bf16[144,768]{1,0:T(8,128)(2,1)S(1)} %collective-permute-done.7.refs_4_), channel_id=1, source_target_pairs={{0,4},{4,0},{1,5},{5,1},{2,6},{6,2},{3,7},{7,3},{8,12},{12,8},{9,1... | collective-permute-start | bytes 663560 | tf_op jit(solution)/shard_map/ppermute | solution.py:424
  60.7 7.1 %collective-permute-start.13 = (bf16[144,768]{1,0:T(8,128)(2,1)}, bf16[144,768]{1,0:T(8,128)(2,1)S(1)}, u32[]{:S(2)}, u32[]{:S(2)}) collective-permute-start(bf16[144,768]{1,0:T(8,128)(2,1)} %collective-permute-done.10.refs_6_), channel_id=1, source_target_pairs={{0,4},{4,0},{1,5},{5,1},{2,6},{6,2},{3,7},{7,3},{8,12},{12,8},{9,1... | collective-permute-start | bytes 663560 | tf_op jit(solution)/shard_map/ppermute | solution.py:424
  70.5 27.7 %copy-start.7 = (bf16[256,1024]{1,0:T(8,128)(2,1)S(1)}, bf16[256,1024]{1,0:T(8,128)(2,1)}, u32[]{:S(2)}) copy-start(bf16[256,1024]{1,0:T(8,128)(2,1)} %refs_3_.1) | copy-start | bytes 1572868
  70.5 27.7 %copy-start.9 = (f32[1024]{0:T(1024)S(1)}, f32[1024]{0:T(1024)}, u32[]{:S(2)}) copy-start(f32[1024]{0:T(1024)} %param.17) | copy-start | bytes 12292
  77.3 31.5 %copy-start.10 = (f32[512]{0:T(512)S(1)}, f32[512]{0:T(512)}, u32[]{:S(2)}) copy-start(f32[512]{0:T(512)} %param.20) | copy-start | bytes 6148
  77.3 31.5 %copy-start.11 = (s32[4,1]{0,1:T(1,128)S(1)}, s32[4,1]{0,1:T(1,128)}, u32[]{:S(2)}) copy-start(s32[4,1]{0,1:T(1,128)} %param.19) | copy-start | bytes 52
  77.3 31.4 %all-to-all-start.2 = ((bf16[64,48,128]{2,1,0:T(8,128)(2,1)}), bf16[64,48,128]{2,1,0:T(8,128)(2,1)S(1)}, u32[]{:S(2)}, u32[]{:S(2)}) async-start(bf16[64,48,128]{2,1,0:T(8,128)(2,1)} %bitcast.11), calls=%async_computation.2 | async-start | bytes 1572864 | tf_op jit(solution)/shard_map/all_to_all | solution.py:492
  86.8 1.0 copy-start.4
  98.3 1.2 %copy-start.5 = (f32[256,1024]{1,0:T(8,128)S(1)}, f32[256,1024]{1,0:T(8,128)}, u32[]{:S(2)}) copy-start(f32[256,1024]{1,0:T(8,128)} %copy-done.4) | copy-start | bytes 3145732

commit v2 on v0

--- a/solution.py
+++ b/solution.py
@@ -453,10 +453,9 @@
     hidden, queries = lax.optimization_barrier((hidden, queries))
     hidden = [hidden] + [shift(hidden, "x", k) for k in range(1, n_x)]
     intra = intra_part(decay_rate, queries, keys, values)
-    hidden[1], intra = lax.optimization_barrier((hidden[1], intra))
     prefix = lax.all_to_all(pieces, CTX, 0, 0, tiled=True).reshape(width, HEAD)
     down = stack_rows([part for pair in zip(down_own, down_other) for part in pair])
-    hidden[2], down = lax.optimization_barrier((hidden[2], down))
+    hidden[2], intra, down = lax.optimization_barrier((hidden[2], intra, down))
     parts = down_part(down, hidden, n_z * n_core, columns)
     parts, prefix = lax.optimization_barrier((parts, prefix))
     parts = parts.reshape(-1, columns, TILE)

time: 110 us -> 109 us (level)
  transfers between devices with their start and end apart: 18 -> 18, of which waited for: 4 -> 5; matrix products, arithmetic and copies ran while one was open for 0% -> 0% of each run, Pallas kernels for 24% -> 24%
where the time goes in v2:
time: 109 us
  starting transfers between devices  43.9 us (40%)
  Pallas kernels  27.6 us (25%)
  waiting for transfers between devices  23.7 us (22%)
  blocking collectives  10.5 us (10%)
  local copies, waits for them, and re-layouts  2.26 us (2%)
    ppermute x15, waiting for transfers between devices, shift(): return lax.ppermute(array, axis, [(i, (i + by) % n) for i in range(n)])  15.6 us
    ppermute x15, starting transfers between devices, shift(): return lax.ppermute(array, axis, [(i, (i + by) % n) for i in range(n)])  14.7 us
    all_to_all x1, starting transfers between devices, on_device(): pieces = lax.all_to_all(pieces, CTX, 0, 0, tiled=True)  12 us
    psum x1, blocking collectives, on_device(): squares = [lax.psum(squares, 'exp')]  10.5 us
    all_to_all x1, starting transfers between devices, on_device(): prefix = lax.all_to_all(pieces, CTX, 0, 0, tiled=True).reshape(width, HEAD)  9.13 us
    all_to_all x1, waiting for transfers between devices, on_device(): parts = lax.all_to_all(parts, ('z', 'core', 'exp'), 0, 0, tiled=True)  8.11 us
    all_to_all x1, starting transfers between devices, on_device(): parts = lax.all_to_all(parts, ('z', 'core', 'exp'), 0, 0, tiled=True)  8.04 us
    pallas_call x1, Pallas kernels, hidden_part(): pl.pallas_call(functools.partial(_hidden_kernel, count), in_specs=[pl.Blo...  7.23 us
  transfers between devices with their start and end apart: 18, of which 5 were waited for; matrix products, arithmetic and copies ran while one was open for 0% of the time, Pallas kernels for 24%

profile of v2, /device:TPU:6, one launch (start us, length us, event | category | flops | bytes accessed | tf_op | source)
XLA Modules:
  0.0 108.8 jit_solution(13284519349630431432)
XLA Ops:
  0.8 0.5 collective-permute-start.2
  1.3 4.4 %pick_tiles.1 = (bf16[128,3072]{1,0:T(8,128)(2,1)}, bf16[128,3072]{1,0:T(8,128)(2,1)}, bf16[128,3072]{1,0:T(8,128)(2,1)}, bf16[128,3072]{1,0:T(8,128)(2,1)}) custom-call(s32[4]{0:T(128)} %bitcast.20, bf16[512,3072]{1,0:T(8,128)(2,1)} %rows.1), custom_call_target="tpu_custom_call" | custom-call | tf_op jit(solution)/shard_map/pick_tiles/pallas_call | solution.py:209
  5.7 1.7 %collective-permute-start = (bf16[128,3072]{1,0:T(8,128)(2,1)}, bf16[128,3072]{1,0:T(8,128)(2,1)}, u32[]{:S(2)}, u32[]{:S(2)}) collective-permute-start(bf16[128,3072]{1,0:T(8,128)(2,1)} %get-tuple-element.40), channel_id=1, source_target_pairs={{0,1},{1,2},{2,3},{3,0},{4,5},{5,6},{6,7},{7,4},{8,9},{9,10},{10,1... | collective-permute-start | bytes 2359304 | tf_op jit(solution)/shard_map/ppermute | solution.py:398
  7.4 2.9 %collective-permute-start.3 = (bf16[128,3072]{1,0:T(8,128)(2,1)}, bf16[128,3072]{1,0:T(8,128)(2,1)}, u32[]{:S(2)}, u32[]{:S(2)}) collective-permute-start(bf16[128,3072]{1,0:T(8,128)(2,1)} %get-tuple-element.45), channel_id=1, source_target_pairs={{0,2},{1,3},{2,0},{3,1},{4,6},{5,7},{6,4},{7,5},{8,10},{9,11},{10,... | collective-permute-start | bytes 2359304 | tf_op jit(solution)/shard_map/ppermute | solution.py:398
  10.3 1.3 %collective-permute-start.4 = (bf16[128,3072]{1,0:T(8,128)(2,1)}, bf16[128,3072]{1,0:T(8,128)(2,1)}, u32[]{:S(2)}, u32[]{:S(2)}) collective-permute-start(bf16[128,3072]{1,0:T(8,128)(2,1)} %get-tuple-element.46), channel_id=1, source_target_pairs={{0,3},{1,0},{2,1},{3,2},{4,7},{5,4},{6,5},{7,6},{8,11},{9,8},{10,9... | collective-permute-start | bytes 2359304 | tf_op jit(solution)/shard_map/ppermute | solution.py:398
  11.6 1.9 %local_states.1 = bf16[1024,128]{1,0:T(8,128)(2,1)} custom-call(f32[8]{0:T(128)S(1)} %copy-done.8, bf16[256,1024]{1,0:T(8,128)(2,1)S(1)} %copy-done, bf16[256,1024]{1,0:T(8,128)(2,1)S(1)} %copy-done.1), custom_call_target="tpu_custom_call" | custom-call | tf_op jit(solution)/shard_map/local_states/pallas_call | solution.py:36
  13.6 12.0 %all-to-all-start = ((bf16[64,16,128]{2,1,0:T(8,128)(2,1)}), bf16[64,16,128]{2,1,0:T(8,128)(2,1)S(1)}, u32[]{:S(2)}, u32[]{:S(2)}) async-start(bf16[64,16,128]{2,1,0:T(8,128)(2,1)} %bitcast.5), calls=%async_computation | async-start | bytes 524288 | tf_op jit(solution)/shard_map/all_to_all | solution.py:430
  25.6 1.9 %split_columns.1 = (bf16[144,768]{1,0:T(8,128)(2,1)S(1)}, bf16[144,768]{1,0:T(8,128)(2,1)S(1)}, bf16[144,768]{1,0:T(8,128)(2,1)}, bf16[144,768]{1,0:T(8,128)(2,1)S(1)}) custom-call(bf16[144,3072]{1,0:T(8,128)(2,1)S(1)} %bitcast.17), custom_call_target="tpu_custom_call" | custom-call | tf_op jit(solution)/shard_map/split_columns/pallas_call | solution.py:295
  27.5 0.5 collective-permute-start.8
  27.9 2.5 %collective-permute-start.6 = (bf16[144,768]{1,0:T(8,128)(2,1)}, bf16[144,768]{1,0:T(8,128)(2,1)S(1)}, u32[]{:S(2)}, u32[]{:S(2)}) collective-permute-start(bf16[144,768]{1,0:T(8,128)(2,1)} %get-tuple-element.53), channel_id=1, source_target_pairs={{0,16},{8,24},{16,0},{24,8},{1,17},{9,25},{17,1},{25,9},{2,18},{10... | collective-permute-start | bytes 663560 | tf_op jit(solution)/shard_map/ppermute | solution.py:398
  30.4 7.2 %collective-permute-done.8.refs_2_ = bf16[144,768]{1,0:T(8,128)(2,1)S(1)} collective-permute-done((bf16[144,768]{1,0:T(8,128)(2,1)S(1)}, bf16[144,768]{1,0:T(8,128)(2,1)S(1)}, u32[]{:S(2)}, u32[]{:S(2)}) %collective-permute-start.8) | collective-permute-done | bytes 221216 | tf_op jit(solution)/shard_map/ppermute | solution.py:398
  37.5 0.6 collective-permute-start.9
  38.2 1.4 %scan_states.1 = bf16[64,16,128]{2,1,0:T(8,128)(2,1)} custom-call(f32[8]{0:T(128)S(1)} %copy-done.8, bf16[64,16,128]{2,1,0:T(8,128)(2,1)S(1)} %all-to-all-done.states), custom_call_target="tpu_custom_call" | custom-call | tf_op jit(solution)/shard_map/scan_states/pallas_call | solution.py:58
  39.6 9.1 %all-to-all-start.1 = ((bf16[64,16,128]{2,1,0:T(8,128)(2,1)}), bf16[64,16,128]{2,1,0:T(8,128)(2,1)S(1)}, u32[]{:S(2)}, u32[]{:S(2)}) async-start(bf16[64,16,128]{2,1,0:T(8,128)(2,1)} %scan_states.1), calls=%async_computation.1 | async-start | bytes 524288 | tf_op jit(solution)/shard_map/all_to_all | solution.py:456
  49.3 7.2 %hidden_part.1.refs_0_ = bf16[288,512]{1,0:T(8,128)(2,1)} custom-call(bf16[128,3072]{1,0:T(8,128)(2,1)} %get-tuple-element.39.refs_0_, bf16[128,3072]{1,0:T(8,128)(2,1)} %collective-permute-done.refs_1_, bf16[128,3072]{1,0:T(8,128)(2,1)} %collective-permute-done.3.refs_2_, bf16[128,3072]{1,0:T(8,128)(2,1)} %collective-permute-done.4.refs_3_, ...), custom_call_target="tpu_custom_call" | custom-call | tf_op jit(solution)/shard_map/hidden_part/pallas_call | solution.py:257
  56.6 1.5 %collective-permute-start.5 = (bf16[288,512]{1,0:T(8,128)(2,1)}, bf16[288,512]{1,0:T(8,128)(2,1)S(1)}, u32[]{:S(2)}, u32[]{:S(2)}) collective-permute-start(bf16[288,512]{1,0:T(8,128)(2,1)} %hidden_part.1.refs_0_), channel_id=1, source_target_pairs={{0,16},{8,24},{16,0},{24,8},{1,17},{9,25},{17,1},{25,9},{2,18},{10... | collective-permute-start | bytes 884744 | tf_op jit(solution)/shard_map/ppermute | solution.py:398
  58.1 2.1 %collective-permute-start.13 = (bf16[288,512]{1,0:T(8,128)(2,1)}, bf16[288,512]{1,0:T(8,128)(2,1)S(1)}, u32[]{:S(2)}, u32[]{:S(2)}) collective-permute-start(bf16[288,512]{1,0:T(8,128)(2,1)} %hidden_part.1.refs_0_), channel_id=1, source_target_pairs={{0,8},{8,16},{16,24},{24,0},{1,9},{9,17},{17,25},{25,1},{2,10},{10... | collective-permute-start | bytes 884744 | tf_op jit(solution)/shard_map/ppermute | solution.py:398
  60.2 0.5 collective-permute-start.12
  60.7 2.0 %intra_part.1.intra = f32[256,1024]{1,0:T(8,128)S(1)} custom-call(f32[8]{0:T(128)S(1)} %copy-done.8, bf16[256,1024]{1,0:T(8,128)(2,1)S(1)} %copy-done.2, bf16[256,1024]{1,0:T(8,128)(2,1)S(1)} %copy-done, bf16[256,1024]{1,0:T(8,128)(2,1)S(1)} %copy-done.1), custom_call_target="tpu_custom_call" | custom-call | tf_op jit(solution)/shard_map/intra_part/pallas_call | solution.py:92
  62.8 2.7 %stack_rows.1.weight = bf16[1152,768]{1,0:T(8,128)(2,1)S(1)} custom-call(bf16[144,768]{1,0:T(8,128)(2,1)S(1)} %get-tuple-element.54.refs_0_, bf16[144,768]{1,0:T(8,128)(2,1)S(1)} %collective-permute-done.7.refs_1_, bf16[144,768]{1,0:T(8,128)(2,1)S(1)} %collective-permute-done.8.refs_2_, bf16[144,768]{1,0:T(8,128)(2,1)S(1)} %collective-permute-done.10.refs_3_, ...), custom_call_target="tpu_custom_call" | custom-call | tf_op jit(solution)/shard_map/stack_rows/pallas_call | solution.py:320
  65.5 2.7 %collective-permute-done.5.refs_2_ = bf16[288,512]{1,0:T(8,128)(2,1)S(1)} collective-permute-done((bf16[288,512]{1,0:T(8,128)(2,1)}, bf16[288,512]{1,0:T(8,128)(2,1)S(1)}, u32[]{:S(2)}, u32[]{:S(2)}) %collective-permute-start.5) | collective-permute-done | bytes 294944 | tf_op jit(solution)/shard_map/ppermute | solution.py:398
  68.3 3.5 %collective-permute-done.13.refs_1_ = bf16[288,512]{1,0:T(8,128)(2,1)S(1)} collective-permute-done((bf16[288,512]{1,0:T(8,128)(2,1)}, bf16[288,512]{1,0:T(8,128)(2,1)S(1)}, u32[]{:S(2)}, u32[]{:S(2)}) %collective-permute-start.13) | collective-permute-done | bytes 294944 | tf_op jit(solution)/shard_map/ppermute | solution.py:398
  71.8 2.1 %collective-permute-done.14.refs_3_ = bf16[288,512]{1,0:T(8,128)(2,1)S(1)} collective-permute-done((bf16[288,512]{1,0:T(8,128)(2,1)}, bf16[288,512]{1,0:T(8,128)(2,1)S(1)}, u32[]{:S(2)}, u32[]{:S(2)}) %collective-permute-start.14) | collective-permute-done | bytes 294944 | tf_op jit(solution)/shard_map/ppermute | solution.py:398
  73.9 2.1 %down_part.1 = bf16[16,4,48,128]{3,2,1,0:T(8,128)(2,1)} custom-call(bf16[1152,768]{1,0:T(8,128)(2,1)S(1)} %stack_rows.1.weight, bf16[288,512]{1,0:T(8,128)(2,1)S(1)} %copy-done.3, bf16[288,512]{1,0:T(8,128)(2,1)S(1)} %collective-permute-done.13.refs_1_, bf16[288,512]{1,0:T(8,128)(2,1)S(1)} %collective-permute-done.5.refs_2_, ...), custom_call_target="tpu_custom_call" | custom-call | tf_op jit(solution)/shard_map/down_part/pallas_call | solution.py:350
  76.1 8.0 %all-to-all-start.2 = ((bf16[64,48,128]{2,1,0:T(8,128)(2,1)}), bf16[64,48,128]{2,1,0:T(8,128)(2,1)S(1)}, u32[]{:S(2)}, u32[]{:S(2)}) async-start(bf16[64,48,128]{2,1,0:T(8,128)(2,1)} %bitcast.9), calls=%async_computation.2 | async-start | bytes 1572864 | tf_op jit(solution)/shard_map/all_to_all | solution.py:462
  84.1 1.3 %mix_part.1 = (f32[256,1024]{1,0:T(8,128)S(1)}, f32[1,256]{1,0:T(1,128)S(1)}) custom-call(f32[8]{0:T(128)S(1)} %copy-done.8, f32[256,1024]{1,0:T(8,128)S(1)} %intra_part.1.intra, bf16[256,1024]{1,0:T(8,128)(2,1)S(1)} %copy-done.2, bf16[1024,128]{1,0:T(8,128)(2,1)S(1)} %bitcast.16), custom_call_target="tpu_custom_call" | custom-call | tf_op jit(solution)/shard_map/mix_part/pallas_call | solution.py:126
  85.5 1.0 copy-done.4
  86.4 10.5 %psum.7.refs_0_ = f32[1,256]{1,0:T(1,128)S(1)} all-reduce(f32[1,256]{1,0:T(1,128)S(1)} %get-tuple-element.65), channel_id=1, replica_groups=mesh['z'=8,'x'=4,'core'=2,'exp'=4] {'exp'}, use_global_device_ids=true, to_apply=%region_0.0 | all-reduce | flops 256 | bytes 2048 | tf_op jit(solution)/shard_map/psum | solution.py:466
  97.0 1.2 %copy-done.5 = f32[256,1024]{1,0:T(8,128)S(1)} copy-done((f32[256,1024]{1,0:T(8,128)S(1)}, f32[256,1024]{1,0:T(8,128)}, u32[]{:S(2)}) %copy-start.5) | copy-done | bytes 1048600
  98.2 1.2 %norm_part.1 = bf16[256,1024]{1,0:T(8,128)(2,1)} custom-call(f32[1,256]{1,0:T(1,128)S(1)} %psum.7.refs_0_, f32[256,1024]{1,0:T(8,128)S(1)} %copy-done.5, f32[1,1024]{1,0:T(1,128)S(1)} %bitcast.18, bf16[256,1024]{1,0:T(8,128)(2,1)S(1)} %copy-done.7), custom_call_target="tpu_custom_call" | custom-call | tf_op jit(solution)/shard_map/norm_part/pallas_call | solution.py:161
  99.4 8.1 %all-to-all-done.2 = bf16[64,48,128]{2,1,0:T(8,128)(2,1)S(1)} async-done(((bf16[64,48,128]{2,1,0:T(8,128)(2,1)}), bf16[64,48,128]{2,1,0:T(8,128)(2,1)S(1)}, u32[]{:S(2)}, u32[]{:S(2)}) %all-to-all-start.2) | async-done | bytes 786464 | tf_op jit(solution)/shard_map/all_to_all | solution.py:462
  107.5 1.3 %finish_part.1 = bf16[48,512]{1,0:T(8,128)(2,1)} custom-call(s32[4]{0:T(128)S(1)} %bitcast.21, bf16[8,2,4,48,128]{4,3,2,1,0:T(8,128)(2,1)S(1)} %bitcast.15, f32[1,512]{1,0:T(1,128)S(1)} %bitcast.19), custom_call_target="tpu_custom_call" | custom-call | tf_op jit(solution)/shard_map/finish_part/pallas_call | solution.py:386
  (42 shorter events, 0.8 us)
Async XLA Ops:
  0.6 11.0 %copy-start = (bf16[256,1024]{1,0:T(8,128)(2,1)S(1)}, bf16[256,1024]{1,0:T(8,128)(2,1)}, u32[]{:S(2)}) copy-start(bf16[256,1024]{1,0:T(8,128)(2,1)} %k.2) | copy-start | bytes 1572868
  0.6 11.0 %copy-start.8 = (f32[8]{0:T(128)S(1)}, f32[8]{0:T(128)}, u32[]{:S(2)}) copy-start(f32[8]{0:T(128)} %rate.7) | copy-start | bytes 100
  0.7 11.0 %copy-start.1 = (bf16[256,1024]{1,0:T(8,128)(2,1)S(1)}, bf16[256,1024]{1,0:T(8,128)(2,1)}, u32[]{:S(2)}) copy-start(bf16[256,1024]{1,0:T(8,128)(2,1)} %v.3) | copy-start | bytes 1572868
  0.7 24.9 %copy-start.6 = (bf16[1,144,3072]{2,1,0:T(8,128)(2,1)S(1)}, bf16[1,144,3072]{2,1,0:T(8,128)(2,1)}, u32[]{:S(2)}) copy-start(bf16[1,144,3072]{2,1,0:T(8,128)(2,1)} %param.23) | copy-start | bytes 2654212
  0.7 10.9 %collective-permute-start.1 = (bf16[144,3072]{1,0:T(8,128)(2,1)}, bf16[144,3072]{1,0:T(8,128)(2,1)S(1)}, u32[]{:S(2)}, u32[]{:S(2)}) collective-permute-start(bf16[144,3072]{1,0:T(8,128)(2,1)} %bitcast.22), channel_id=1, source_target_pairs={{0,4},{4,0},{1,5},{5,1},{2,6},{6,2},{3,7},{7,3},{8,12},{12,8},{9,1... | collective-permute-start | bytes 2654216 | tf_op jit(solution)/shard_map/ppermute | solution.py:398
  0.8 10.8 %collective-permute-start.2 = (bf16[144,3072]{1,0:T(8,128)(2,1)}, bf16[144,3072]{1,0:T(8,128)(2,1)}, u32[]{:S(2)}, u32[]{:S(2)}) collective-permute-start(bf16[144,3072]{1,0:T(8,128)(2,1)} %bitcast.24), channel_id=1, source_target_pairs={{0,4},{4,0},{1,5},{5,1},{2,6},{6,2},{3,7},{7,3},{8,12},{12,8},{9,1... | collective-permute-start | bytes 2654216 | tf_op jit(solution)/shard_map/ppermute | solution.py:398
  5.7 43.6 %collective-permute-start = (bf16[128,3072]{1,0:T(8,128)(2,1)}, bf16[128,3072]{1,0:T(8,128)(2,1)}, u32[]{:S(2)}, u32[]{:S(2)}) collective-permute-start(bf16[128,3072]{1,0:T(8,128)(2,1)} %get-tuple-element.40), channel_id=1, source_target_pairs={{0,1},{1,2},{2,3},{3,0},{4,5},{5,6},{6,7},{7,4},{8,9},{9,10},{10,1... | collective-permute-start | bytes 2359304 | tf_op jit(solution)/shard_map/ppermute | solution.py:398
  7.4 42.0 %collective-permute-start.3 = (bf16[128,3072]{1,0:T(8,128)(2,1)}, bf16[128,3072]{1,0:T(8,128)(2,1)}, u32[]{:S(2)}, u32[]{:S(2)}) collective-permute-start(bf16[128,3072]{1,0:T(8,128)(2,1)} %get-tuple-element.45), channel_id=1, source_target_pairs={{0,2},{1,3},{2,0},{3,1},{4,6},{5,7},{6,4},{7,5},{8,10},{9,11},{10,... | collective-permute-start | bytes 2359304 | tf_op jit(solution)/shard_map/ppermute | solution.py:398
  10.3 39.1 %collective-permute-start.4 = (bf16[128,3072]{1,0:T(8,128)(2,1)}, bf16[128,3072]{1,0:T(8,128)(2,1)}, u32[]{:S(2)}, u32[]{:S(2)}) collective-permute-start(bf16[128,3072]{1,0:T(8,128)(2,1)} %get-tuple-element.46), channel_id=1, source_target_pairs={{0,3},{1,0},{2,1},{3,2},{4,7},{5,4},{6,5},{7,6},{8,11},{9,8},{10,9... | collective-permute-start | bytes 2359304 | tf_op jit(solution)/shard_map/ppermute | solution.py:398
  11.6 13.9 %copy-start.12 = (bf16[144,3072]{1,0:T(8,128)(2,1)}, bf16[144,3072]{1,0:T(8,128)(2,1)S(1)}, u32[]{:S(2)}) copy-start(bf16[144,3072]{1,0:T(8,128)(2,1)S(1)} %collective-permute-done.1.refs_5_) | copy-start | bytes 2654212
  13.6 24.6 %all-to-all-start = ((bf16[64,16,128]{2,1,0:T(8,128)(2,1)}), bf16[64,16,128]{2,1,0:T(8,128)(2,1)S(1)}, u32[]{:S(2)}, u32[]{:S(2)}) async-start(bf16[64,16,128]{2,1,0:T(8,128)(2,1)} %bitcast.5), calls=%async_computation | async-start | bytes 524288 | tf_op jit(solution)/shard_map/all_to_all | solution.py:430
  27.5 10.1 %collective-permute-start.8 = (bf16[144,768]{1,0:T(8,128)(2,1)S(1)}, bf16[144,768]{1,0:T(8,128)(2,1)S(1)}, u32[]{:S(2)}, u32[]{:S(2)}) collective-permute-start(bf16[144,768]{1,0:T(8,128)(2,1)S(1)} %get-tuple-element.55), channel_id=1, source_target_pairs={{0,8},{8,16},{16,24},{24,0},{1,9},{9,17},{17,25},{25,1},{2,10},{10... | collective-permute-start | bytes 663560 | tf_op jit(solution)/shard_map/ppermute | solution.py:398
  27.9 20.8 %collective-permute-start.6 = (bf16[144,768]{1,0:T(8,128)(2,1)}, bf16[144,768]{1,0:T(8,128)(2,1)S(1)}, u32[]{:S(2)}, u32[]{:S(2)}) collective-permute-start(bf16[144,768]{1,0:T(8,128)(2,1)} %get-tuple-element.53), channel_id=1, source_target_pairs={{0,16},{8,24},{16,0},{24,8},{1,17},{9,25},{17,1},{25,9},{2,18},{10... | collective-permute-start | bytes 663560 | tf_op jit(solution)/shard_map/ppermute | solution.py:398
  37.5 11.4 %collective-permute-start.9 = (bf16[144,768]{1,0:T(8,128)(2,1)S(1)}, bf16[144,768]{1,0:T(8,128)(2,1)}, u32[]{:S(2)}, u32[]{:S(2)}) collective-permute-start(bf16[144,768]{1,0:T(8,128)(2,1)S(1)} %get-tuple-element.57), channel_id=1, source_target_pairs={{0,24},{8,0},{16,8},{24,16},{1,25},{9,1},{17,9},{25,17},{2,26},{10... | collective-permute-start | bytes 663560 | tf_op jit(solution)/shard_map/ppermute | solution.py:398
  39.6 36.5 %all-to-all-start.1 = ((bf16[64,16,128]{2,1,0:T(8,128)(2,1)}), bf16[64,16,128]{2,1,0:T(8,128)(2,1)S(1)}, u32[]{:S(2)}, u32[]{:S(2)}) async-start(bf16[64,16,128]{2,1,0:T(8,128)(2,1)} %scan_states.1), calls=%async_computation.1 | async-start | bytes 524288 | tf_op jit(solution)/shard_map/all_to_all | solution.py:456
  48.7 12.0 %copy-start.2 = (bf16[256,1024]{1,0:T(8,128)(2,1)S(1)}, bf16[256,1024]{1,0:T(8,128)(2,1)}, u32[]{:S(2)}) copy-start(bf16[256,1024]{1,0:T(8,128)(2,1)} %q.1) | copy-start | bytes 1572868
  48.7 11.5 %collective-permute-start.7 = (bf16[144,768]{1,0:T(8,128)(2,1)S(1)}, bf16[144,768]{1,0:T(8,128)(2,1)S(1)}, u32[]{:S(2)}, u32[]{:S(2)}) collective-permute-start(bf16[144,768]{1,0:T(8,128)(2,1)S(1)} %get-tuple-element.54.refs_0_), channel_id=1, source_target_pairs={{0,4},{4,0},{1,5},{5,1},{2,6},{6,2},{3,7},{7,3},{8,12},{12,8},{9,1... | collective-permute-start | bytes 663560 | tf_op jit(solution)/shard_map/ppermute | solution.py:398
  49.0 11.3 %collective-permute-start.10 = (bf16[144,768]{1,0:T(8,128)(2,1)S(1)}, bf16[144,768]{1,0:T(8,128)(2,1)S(1)}, u32[]{:S(2)}, u32[]{:S(2)}) collective-permute-start(bf16[144,768]{1,0:T(8,128)(2,1)S(1)} %collective-permute-done.8.refs_2_), channel_id=1, source_target_pairs={{0,4},{4,0},{1,5},{5,1},{2,6},{6,2},{3,7},{7,3},{8,12},{12,8},{9,1... | collective-permute-start | bytes 663560 | tf_op jit(solution)/shard_map/ppermute | solution.py:398
  56.6 17.4 %copy-start.3 = (bf16[288,512]{1,0:T(8,128)(2,1)S(1)}, bf16[288,512]{1,0:T(8,128)(2,1)}, u32[]{:S(2)}) copy-start(bf16[288,512]{1,0:T(8,128)(2,1)} %hidden_part.1.refs_0_) | copy-start | bytes 884740
  56.6 11.7 %collective-permute-start.5 = (bf16[288,512]{1,0:T(8,128)(2,1)}, bf16[288,512]{1,0:T(8,128)(2,1)S(1)}, u32[]{:S(2)}, u32[]{:S(2)}) collective-permute-start(bf16[288,512]{1,0:T(8,128)(2,1)} %hidden_part.1.refs_0_), channel_id=1, source_target_pairs={{0,16},{8,24},{16,0},{24,8},{1,17},{9,25},{17,1},{25,9},{2,18},{10... | collective-permute-start | bytes 884744 | tf_op jit(solution)/shard_map/ppermute | solution.py:398
  58.1 13.6 %collective-permute-start.13 = (bf16[288,512]{1,0:T(8,128)(2,1)}, bf16[288,512]{1,0:T(8,128)(2,1)S(1)}, u32[]{:S(2)}, u32[]{:S(2)}) collective-permute-start(bf16[288,512]{1,0:T(8,128)(2,1)} %hidden_part.1.refs_0_), channel_id=1, source_target_pairs={{0,8},{8,16},{16,24},{24,0},{1,9},{9,17},{17,25},{25,1},{2,10},{10... | collective-permute-start | bytes 884744 | tf_op jit(solution)/shard_map/ppermute | solution.py:398
  60.2 13.7 %collective-permute-start.14 = (bf16[288,512]{1,0:T(8,128)(2,1)}, bf16[288,512]{1,0:T(8,128)(2,1)S(1)}, u32[]{:S(2)}, u32[]{:S(2)}) collective-permute-start(bf16[288,512]{1,0:T(8,128)(2,1)} %hidden_part.1.refs_0_), channel_id=1, source_target_pairs={{0,24},{8,0},{16,8},{24,16},{1,25},{9,1},{17,9},{25,17},{2,26},{10... | collective-permute-start | bytes 884744 | tf_op jit(solution)/shard_map/ppermute | solution.py:398
  60.2 2.5 %collective-permute-start.11 = (bf16[144,768]{1,0:T(8,128)(2,1)S(1)}, bf16[144,768]{1,0:T(8,128)(2,1)S(1)}, u32[]{:S(2)}, u32[]{:S(2)}) collective-permute-start(bf16[144,768]{1,0:T(8,128)(2,1)S(1)} %collective-permute-done.6.refs_4_), channel_id=1, source_target_pairs={{0,4},{4,0},{1,5},{5,1},{2,6},{6,2},{3,7},{7,3},{8,12},{12,8},{9,1... | collective-permute-start | bytes 663560 | tf_op jit(solution)/shard_map/ppermute | solution.py:398
  60.2 2.5 %collective-permute-start.12 = (bf16[144,768]{1,0:T(8,128)(2,1)}, bf16[144,768]{1,0:T(8,128)(2,1)S(1)}, u32[]{:S(2)}, u32[]{:S(2)}) collective-permute-start(bf16[144,768]{1,0:T(8,128)(2,1)} %collective-permute-done.9.refs_6_), channel_id=1, source_target_pairs={{0,4},{4,0},{1,5},{5,1},{2,6},{6,2},{3,7},{7,3},{8,12},{12,8},{9,1... | collective-permute-start | bytes 663560 | tf_op jit(solution)/shard_map/ppermute | solution.py:398
  65.5 31.4 %copy-start.7 = (bf16[256,1024]{1,0:T(8,128)(2,1)S(1)}, bf16[256,1024]{1,0:T(8,128)(2,1)}, u32[]{:S(2)}) copy-start(bf16[256,1024]{1,0:T(8,128)(2,1)} %refs_3_.1) | copy-start | bytes 1572868
  65.5 31.4 %copy-start.9 = (f32[1024]{0:T(1024)S(1)}, f32[1024]{0:T(1024)}, u32[]{:S(2)}) copy-start(f32[1024]{0:T(1024)} %param.17) | copy-start | bytes 12292
  76.0 31.4 %copy-start.10 = (f32[512]{0:T(512)S(1)}, f32[512]{0:T(512)}, u32[]{:S(2)}) copy-start(f32[512]{0:T(512)} %param.20) | copy-start | bytes 6148
  76.0 31.4 %copy-start.11 = (s32[4,1]{0,1:T(1,128)S(1)}, s32[4,1]{0,1:T(1,128)}, u32[]{:S(2)}) copy-start(s32[4,1]{0,1:T(1,128)} %param.19) | copy-start | bytes 52
  76.1 31.4 %all-to-all-start.2 = ((bf16[64,48,128]{2,1,0:T(8,128)(2,1)}), bf16[64,48,128]{2,1,0:T(8,128)(2,1)S(1)}, u32[]{:S(2)}, u32[]{:S(2)}) async-start(bf16[64,48,128]{2,1,0:T(8,128)(2,1)} %bitcast.9), calls=%async_computation.2 | async-start | bytes 1572864 | tf_op jit(solution)/shard_map/all_to_all | solution.py:462
  85.5 1.0 copy-start.4
  97.0 1.2 %copy-start.5 = (f32[256,1024]{1,0:T(8,128)S(1)}, f32[256,1024]{1,0:T(8,128)}, u32[]{:S(2)}) copy-start(f32[256,1024]{1,0:T(8,128)} %copy-done.4) | copy-start | bytes 3145732
